TPU v7x, 256 devices: a whole 4x4x8 slice. The times are simulated.
256 devices in a mesh: outer: 8 (over y, z_lo), inner: 32 (over z_hi, x, core).
Axes of the slice: x: 4, y: 4, z: 8 (z_hi: 4, z_lo: 2; z = z_hi * 2 + z_lo), core: 2. Of those that a mesh axis runs over, the one named last changes fastest.
Arguments:
- queries: bfloat16 [32768, 384], P(('outer', 'inner')), may hold values from -6 to 6
- key_rows: bfloat16 [32768, 128], P(('outer', 'inner')), may hold values from -6 to 6
- value_rows: bfloat16 [32768, 128], P(('outer', 'inner')), may hold values from -6 to 6
- grad_output: bfloat16 [32768, 384], P(('outer', 'inner')), may hold values from -6 to 6
- segments: int32 [32768], replicated, may hold values from 0 to 31, never falling along the last dimension, each value on 1 to 2048 neighbouring positions
Outputs:
- grad_queries: bfloat16 [32768, 384], P(('outer', 'inner'))
- grad_keys: bfloat16 [32768, 128], P(('outer', 'inner'))
- grad_values: bfloat16 [32768, 128], P(('outer', 'inner'))
Inputs may be any that keep to these rules, and one draw needn't show every extreme that they name: `segments`: ids never fall; each document has 1 to 2048 tokens and one has exactly 2048.
All inputs are finite; a program needn't handle non-finite values.
Results may differ from a plain program's by a relative error of at most 0.009.
Values may be sent and summed in bfloat16 or wider, within the bound.
A program may use at most 64 MiB of HBM per device.

v0:
```python
import jax
import jax.numpy as jnp
from jax import lax
from jax.sharding import PartitionSpec as P

NEGATIVE = -1e30


def passed_along(shard, axis, by):
    devices = lax.axis_size(axis)
    pairs = [(i, i + by) for i in range(devices) if 0 <= i + by < devices]
    return lax.ppermute(shard, axis, pairs)


def tile_forward(softmax_state, query_half, grad_half, key_tile, value_tile, allowed, score_scale):

    def active(current):
        run_max, run_total, run_delta = current
        scores = (
            jnp.einsum("qhd,kd->hqk", query_half, key_tile, preferred_element_type=jnp.float32)
            * score_scale
        )
        masked = jnp.where(allowed[None], scores, NEGATIVE)
        new_max = jnp.maximum(run_max, jnp.max(masked, axis=2))
        weights = jnp.where(allowed[None], jnp.exp(scores - new_max[:, :, None]), 0.0)
        slopes = jnp.einsum(
            "qhd,kd->hqk", grad_half, value_tile, preferred_element_type=jnp.float32
        )
        factor = jnp.exp(run_max - new_max)
        return (
            new_max,
            run_total * factor + jnp.sum(weights, axis=2),
            run_delta * factor + jnp.sum(weights * slopes, axis=2),
        )

    def passed(current):
        return current

    return lax.cond(jnp.any(allowed), active, passed, softmax_state)


def tile_backward(
    query_half, grad_half, key_tile, value_tile, allowed, log_total, delta_rows, score_scale
):

    def active(operands):
        key_part, value_part = operands
        scores = (
            jnp.einsum("qhd,kd->hqk", query_half, key_part, preferred_element_type=jnp.float32)
            * score_scale
        )
        attn_probs = jnp.where(allowed[None], jnp.exp(scores - log_total[:, :, None]), 0.0)
        slopes = jnp.einsum(
            "qhd,kd->hqk", grad_half, value_part, preferred_element_type=jnp.float32
        )
        grad_scores = attn_probs * (slopes - delta_rows[:, :, None])
        probs_low = attn_probs.astype(jnp.bfloat16)
        grad_low = grad_scores.astype(jnp.bfloat16)
        add_query = (
            jnp.einsum("hqk,kd->qhd", grad_low, key_part, preferred_element_type=jnp.float32)
            * score_scale
        )
        grad_key = (
            jnp.einsum("hqk,qhd->kd", grad_low, query_half, preferred_element_type=jnp.float32)
            * score_scale
        )
        grad_value = jnp.einsum(
            "hqk,qhd->kd", probs_low, grad_half, preferred_element_type=jnp.float32
        )
        return (add_query, grad_key, grad_value)

    def skipped(operands):
        key_part, value_part = operands
        return (
            jnp.zeros(query_half.shape, jnp.float32),
            jnp.zeros(key_part.shape, jnp.float32),
            jnp.zeros(value_part.shape, jnp.float32),
        )

    return lax.cond(jnp.any(allowed), active, skipped, (key_tile, value_tile))


def local(queries, key_rows, value_rows, grad_output, segments):
    local_rows = key_rows.shape[0]
    span_rows = local_rows // 2
    head_width = key_rows.shape[1]
    head_count = queries.shape[1] // head_width
    score_scale = head_width ** (-0.5)
    inner_count = lax.axis_size("inner")
    outer_count = lax.axis_size("outer")
    devices = inner_count * outer_count
    outer_index = lax.axis_index("outer")
    inner_index = lax.axis_index("inner")
    my_index = outer_index * inner_count + inner_index
    offsets = jnp.arange(span_rows, dtype=jnp.int32)
    front_pos = my_index * span_rows + offsets
    back_pos = (2 * devices - 1 - my_index) * span_rows + offsets
    query_pos = jnp.stack([front_pos, back_pos])
    query_seg = jnp.take(segments, query_pos)
    query_split = queries.reshape(2, span_rows, head_count, head_width)
    grad_split = grad_output.reshape(2, span_rows, head_count, head_width)
    front_pair = jnp.concatenate([key_rows[:span_rows], value_rows[:span_rows]], axis=1)
    back_pair = jnp.concatenate([key_rows[span_rows:], value_rows[span_rows:]], axis=1)
    from_below = passed_along(front_pair, "outer", 1)
    from_above = passed_along(back_pair, "outer", -1)
    stacked = jnp.stack([front_pair, back_pair, from_below, from_above])[:, None]
    gathered = lax.all_gather(stacked, "inner", axis=1, tiled=True)
    slot_shift = jnp.array([0, 0, -1, 1], jnp.int32)
    slot_back = jnp.array([0, 1, 0, 1], jnp.int32)
    source_group = outer_index + slot_shift
    shard_ids = jnp.arange(inner_count, dtype=jnp.int32)
    source_dev = source_group[:, None] * inner_count + shard_ids[None, :]
    span_ids = jnp.where(slot_back[:, None] == 1, 2 * devices - 1 - source_dev, source_dev)
    key_pos = span_ids[:, :, None] * span_rows + offsets[None, None, :]
    valid_slot = (source_group >= 0) & (source_group < outer_count)
    looked_up = jnp.take(segments, jnp.clip(key_pos, 0, segments.shape[0] - 1))
    key_seg = jnp.where(valid_slot[:, None, None], looked_up, -1)
    shards_per_tile = 8
    tile_count = 4 * inner_count // shards_per_tile
    tile_rows = shards_per_tile * span_rows
    key_tiles = gathered.reshape(tile_count, tile_rows, 2 * head_width)
    tile_pos = key_pos.reshape(tile_count, tile_rows)
    tile_seg = key_seg.reshape(tile_count, tile_rows)

    def tile_masks(pos_row, seg_row):
        return [
            (seg_row[None, :] == query_seg[part_index][:, None])
            & (pos_row[None, :] <= query_pos[part_index][:, None])
            for part_index in range(2)
        ]

    zero_rows = jnp.zeros((head_count, span_rows), jnp.float32)
    start_state = (jnp.full((head_count, span_rows), NEGATIVE, jnp.float32), zero_rows, zero_rows)

    def forward_step(states, inputs):
        key_tile, pos_row, seg_row = inputs
        allowed = tile_masks(pos_row, seg_row)
        updated = tuple(
            (
                tile_forward(
                    states[part_index],
                    query_split[part_index],
                    grad_split[part_index],
                    key_tile[:, :head_width],
                    key_tile[:, head_width:],
                    allowed[part_index],
                    score_scale,
                )
                for part_index in range(2)
            )
        )
        return (updated, None)

    final_states, unused = lax.scan(
        forward_step, (start_state, start_state), (key_tiles, tile_pos, tile_seg)
    )
    log_totals = [
        final_states[part_index][0] + jnp.log(final_states[part_index][1])
        for part_index in range(2)
    ]
    delta_list = [
        final_states[part_index][2] / final_states[part_index][1] for part_index in range(2)
    ]

    def backward_step(grad_sum, inputs):
        key_tile, pos_row, seg_row = inputs
        allowed = tile_masks(pos_row, seg_row)
        key_part = key_tile[:, :head_width]
        value_part = key_tile[:, head_width:]
        key_total = jnp.zeros((tile_rows, head_width), jnp.float32)
        value_total = jnp.zeros((tile_rows, head_width), jnp.float32)
        query_adds = []
        for part_index in range(2):
            add_query, grad_key, grad_value = tile_backward(
                query_split[part_index],
                grad_split[part_index],
                key_part,
                value_part,
                allowed[part_index],
                log_totals[part_index],
                delta_list[part_index],
                score_scale,
            )
            query_adds.append(add_query)
            key_total = key_total + grad_key
            value_total = value_total + grad_value
        return (grad_sum + jnp.stack(query_adds), jnp.concatenate([key_total, value_total], axis=1))

    query_start = jnp.zeros((2, span_rows, head_count, head_width), jnp.float32)
    grad_q, term_tiles = lax.scan(backward_step, query_start, (key_tiles, tile_pos, tile_seg))
    terms = term_tiles.reshape(4, inner_count, span_rows, 2 * head_width)
    summed = lax.psum_scatter(terms, "inner", scatter_dimension=1, tiled=True)
    returned_front = passed_along(summed[2, 0].astype(jnp.bfloat16), "outer", -1).astype(
        jnp.float32
    )
    returned_back = passed_along(summed[3, 0].astype(jnp.bfloat16), "outer", 1).astype(jnp.float32)
    front_total = summed[0, 0] + returned_front
    back_total = summed[1, 0] + returned_back
    grad_total = jnp.concatenate([front_total, back_total], axis=0)
    grad_queries = grad_q.reshape(local_rows, head_count * head_width).astype(jnp.bfloat16)
    return (
        grad_queries,
        grad_total[:, :head_width].astype(jnp.bfloat16),
        grad_total[:, head_width:].astype(jnp.bfloat16),
    )


def solution(mesh):
    placed = (
        P(("outer", "inner"), None),
        P(("outer", "inner"), None),
        P(("outer", "inner"), None),
        P(("outer", "inner"), None),
        P(),
    )
    return jax.shard_map(
        local,
        mesh=mesh,
        in_specs=placed,
        out_specs=(
            P(("outer", "inner"), None),
            P(("outer", "inner"), None),
            P(("outer", "inner"), None),
        ),
        check_vma=False,
    )
```

profile of v0, /device:TPU:8, one launch (start us, length us, event | category | flops | bytes accessed | tf_op | source)
XLA Modules:
  0.0 564.9 jit_solution(5722862292119766887)
XLA Ops:
  8.0 3.7 collective-permute-start.1
  11.8 2.1 collective-permute-start
  13.9 4.6 collective-permute-done
  21.7 45.5 %gather_fusion = s32[8192]{0:T(1024)S(1)} fusion(s32[32768]{0:T(1024)S(1)} %copy-done, s32[8192]{0:T(1024)S(1)} %broadcast_clamp_fusion), kind=kCustom, calls=%fused_computation | custom fusion | bytes 98304 | tf_op jit(solution)/shard_map/jit(_take)/gather | solution.py:116
  67.6 1.1 gather_fusion.1
  69.0 12.8 %all-gather.3.cloned.1.call-done = bf16[4,2048,256]{2,1,0:T(8,128)(2,1)} async-done(((bf16[4,64,256]{2,1,0:T(8,128)(2,1)}), bf16[4,2048,256]{2,1,0:T(8,128)(2,1)}) %all-gather.3.cloned.1.call-update) | async-done | bytes 4194320 | tf_op jit(solution)/shard_map/all_gather | solution.py:107
  81.8 57.5 %while.34 = (s32[]{:T(128)}, f32[3,64]{1,0:T(4,128)S(1)}, f32[3,64]{1,0:T(4,128)S(1)}, f32[3,64]{1,0:T(4,128)S(1)}, f32[3,64]{1,0:T(4,128)S(1)}, /*index=5*/f32[...) while((s32[]{:T(128)}, f32[3,64]{1,0:T(4,128)S(1)}, ...), condition=%wide.region_13.14_spmd.clone, body=%wide.region_0.13_spmd.clone.sunk | while | flops 102892800 | bytes 4436393 | solution.py:154
  87.5 1.0 dynamic-slice_bitcast_fusion.6
  97.3 1.0 dynamic-slice_bitcast_fusion.6
  104.7 1.0 dynamic-slice_bitcast_fusion.6
  115.4 1.0 dynamic-slice_bitcast_fusion.6
  119.5 1.0 dynamic-slice_bitcast_fusion.6
  123.7 1.0 dynamic-slice_bitcast_fusion.6
  131.1 1.0 dynamic-slice_bitcast_fusion.6
  137.6 1.0 dynamic-slice_bitcast_fusion.6
  139.3 75.1 %while.35 = (s32[]{:T(128)}, f32[2,64,3,128]{3,1,2,0:T(8,128)S(1)}, f32[16,512,256]{2,1,0:T(8,128)}, s32[16,512]{1,0:T(8,128)S(1)}, s32[2,64]{1,0:T(2,128)S(1)},...) while((s32[]{:T(128)}, f32[2,64,3,128]{3,1,2,0:T(8,128)S(1)}, ...), condition=%wide.region_21.22_spmd.clone, body=%wide.region_14.21_spmd.clone.sunk | while | flops 253886592 | bytes 10378095 | solution.py:190
  142.5 1.2 conditional.15
  146.2 1.0 dynamic-slice_bitcast_fusion.7
  160.0 1.2 conditional.14
  164.4 1.0 dynamic-slice_bitcast_fusion.7
  172.9 1.0 dynamic-slice_bitcast_fusion.7
  177.2 1.0 dynamic-slice_bitcast_fusion.7
  178.9 1.2 conditional.15
  184.3 1.2 conditional.15
  189.7 1.2 conditional.15
  195.2 1.2 conditional.15
  215.7 325.8 %all-reduce.3.cloned.1.call-done = f32[4,32,64,256]{3,2,1,0:T(8,128)} async-done(((f32[4,32,64,256]{3,2,1,0:T(8,128)}), f32[4,32,64,256]{3,2,1,0:T(8,128)}) %all-reduce.3.cloned.1.call-update) | async-done | bytes 8388624
  541.5 1.6 dynamic-slice_convert_fusion
  543.1 6.0 %collective-permute-start.2 = (bf16[64,256]{1,0:T(8,128)(2,1)S(1)}, bf16[64,256]{1,0:T(8,128)(2,1)S(1)}, u32[]{:S(2)}, u32[]{:S(2)}) collective-permute-start(bf16[64,256]{1,0:T(8,128)(2,1)S(1)} %get-tuple-element.562), channel_id=1, source_target_pairs={{32,0},{64,32},{96,64},{128,96},{160,128},{192,160},{224,192},{33,... | collective-permute-start | bytes 98312 | tf_op jit(solution)/shard_map/ppermute | solution.py:12
  549.1 1.9 collective-permute-start.3
  551.8 4.0 collective-permute-done.3
  555.8 1.5 fusion.72
  (504 shorter events, 91.0 us)
Async XLA Ops:
  7.2 14.5 %copy-start = (s32[32768]{0:T(1024)S(1)}, s32[32768]{0:T(1024)}, u32[]{:S(2)}) copy-start(s32[32768]{0:T(1024)} %param.23) | copy-start | bytes 393220
  7.2 74.6 %all-gather.3.cloned.1.call-start = ((), (), s32[]{:S(2)}) async-start(), calls=%async_computation | async-start | bytes 4325376 | tf_op jit(solution)/shard_map/all_gather | solution.py:107
  8.0 5.9 %collective-permute-start.1 = (bf16[64,256]{1,0:T(8,128)(2,1)S(1)}, bf16[64,256]{1,0:T(8,128)(2,1)S(1)}, u32[]{:S(2)}, u32[]{:S(2)}) collective-permute-start(bf16[64,256]{1,0:T(8,128)(2,1)S(1)} %get-tuple-element.569), channel_id=1, source_target_pairs={{32,0},{64,32},{96,64},{128,96},{160,128},{192,160},{224,192},{33,... | collective-permute-start | bytes 98312 | tf_op jit(solution)/shard_map/ppermute | solution.py:12
  11.8 6.7 %collective-permute-start = (bf16[64,256]{1,0:T(8,128)(2,1)S(1)}, bf16[64,256]{1,0:T(8,128)(2,1)S(1)}, u32[]{:S(2)}, u32[]{:S(2)}) collective-permute-start(bf16[64,256]{1,0:T(8,128)(2,1)S(1)} %get-tuple-element.567), channel_id=1, source_target_pairs={{0,32},{32,64},{64,96},{96,128},{128,160},{160,192},{192,224},{1,3... | collective-permute-start | bytes 98312 | tf_op jit(solution)/shard_map/ppermute | solution.py:12
  19.2 522.3 %all-reduce.3.cloned.1.call-start = ((), (), s32[]{:S(2)}) async-start(), calls=%async_computation.1 | async-start | bytes 16777216
  21.7 47.1 %copy-start.1 = (bf16[128,384]{1,0:T(8,128)(2,1)S(1)}, bf16[128,384]{1,0:T(8,128)(2,1)}, u32[]{:S(2)}) copy-start(bf16[128,384]{1,0:T(8,128)(2,1)} %param.19) | copy-start | bytes 294916
  21.7 47.2 %copy-start.2 = (bf16[128,384]{1,0:T(8,128)(2,1)S(1)}, bf16[128,384]{1,0:T(8,128)(2,1)}, u32[]{:S(2)}) copy-start(bf16[128,384]{1,0:T(8,128)(2,1)} %param.22) | copy-start | bytes 294916
  214.5 0.7 copy-start.3
  543.1 8.7 %collective-permute-start.2 = (bf16[64,256]{1,0:T(8,128)(2,1)S(1)}, bf16[64,256]{1,0:T(8,128)(2,1)S(1)}, u32[]{:S(2)}, u32[]{:S(2)}) collective-permute-start(bf16[64,256]{1,0:T(8,128)(2,1)S(1)} %get-tuple-element.562), channel_id=1, source_target_pairs={{32,0},{64,32},{96,64},{128,96},{160,128},{192,160},{224,192},{33,... | collective-permute-start | bytes 98312 | tf_op jit(solution)/shard_map/ppermute | solution.py:12
  549.1 6.7 %collective-permute-start.3 = (bf16[64,256]{1,0:T(8,128)(2,1)S(1)}, bf16[64,256]{1,0:T(8,128)(2,1)S(1)}, u32[]{:S(2)}, u32[]{:S(2)}) collective-permute-start(bf16[64,256]{1,0:T(8,128)(2,1)S(1)} %get-tuple-element.563), channel_id=1, source_target_pairs={{0,32},{32,64},{64,96},{96,128},{128,160},{160,192},{192,224},{1,3... | collective-permute-start | bytes 98312 | tf_op jit(solution)/shard_map/ppermute | solution.py:12
Sparse Core Ops, SparseCore 0:
  19.3 62.4 all-gather.2
  214.6 326.8 all-reduce.2
where the time goes:
time: 567 us; the launch traced here: 565 us
  waiting for transfers between devices  347 us (61%)
  local copies, waits for them, and re-layouts  85.9 us (15%)
  other arithmetic  47.9 us (8%)
  loops' own time  45.1 us (8%)
  between operations  14.3 us (3%)
  starting transfers between devices  13.8 us (2%)
  matrix products  10.7 us (2%)
    unnamed x3, waiting for transfers between devices  326 us
    gather x2, local copies, waits for them, and re-layouts, local(): looked_up = jnp.take(segments, jnp.clip(key_pos, 0, segments.shape[0] - 1))  45.5 us
    squeeze x32, local copies, waits for them, and re-layouts, local(): lax.scan(forward_step, (start_state, start_state), (key_tiles, tile_pos,...  31.2 us
    another operation x1, loops' own time, local(): lax.scan(forward_step, (start_state, start_state), (key_tiles, tile_pos,...  21.9 us
    another operation x1, loops' own time, local(): lax.scan(backward_step, query_start, (key_tiles, tile_pos, tile_seg))  21.2 us
    ppermute x4, starting transfers between devices, passed_along(): return lax.ppermute(shard, axis, pairs)  13.8 us
    reduce_or x16, other arithmetic, tile_forward(): return lax.cond(jnp.any(allowed), active, passed, softmax_state)  13.5 us
    dynamic_update_slice x16, other arithmetic, local(): lax.scan(backward_step, query_start, (key_tiles, tile_pos, tile_seg))  13.5 us
  transfers between devices with their start and end apart: 6, of which 4 were waited for; matrix products, arithmetic and copies ran while one was open for 9% of the time, Pallas kernels for 0%

commit v1 on v0

v1 whole, which is shorter than its diff:
```python
import functools
import math

import jax
import jax.numpy as jnp
from jax import lax
from jax.experimental import pallas as pl
from jax.experimental.pallas import tpu as pltpu
from jax.sharding import PartitionSpec as P

MESH = pl.DeviceIdType.MESH
NEGATIVE = -1e30
HD = 128
HEADS = 3
SPAN = 64
CHUNK = 512
WINDOW = 5
QTILE = 256
QSTEPS = HEADS * (CHUNK // QTILE)
SCALE = HD**-0.5
KAPPA = SCALE * math.log2(math.e)
f32 = jnp.float32
bf16 = jnp.bfloat16


def dot(a, b, dims):
    return lax.dot_general(a, b, ((dims[0], dims[1]), ((), ())), preferred_element_type=f32)


def kernel(
    slabs_per_group,
    slabs,
    docs,
    q_hbm,
    k_hbm,
    v_hbm,
    g_hbm,
    seg_hbm,
    dq_out,
    dk_out,
    dv_out,
    qd,
    qd_other,
    kv,
    kv_other,
    seg,
    bias,
    e_buf,
    dp_buf,
    ds_buf,
    stat,
    dq_send,
    dq_recv,
    dkv_own,
    dkv_send,
    dkv_recv,
    fin_send,
    fin_recv,
    local_sem,
    seg_sem,
    qd_send_sem,
    qd_recv_sem,
    swap_send_sem,
    swap_recv_sem,
    kv_send_sem,
    kv_recv_sem,
    stat_send_sem,
    stat_recv_sem,
    dq_send_sem,
    dq_recv_sem,
    dkv_send_sem,
    dkv_recv_sem,
    fin_send_sem,
    fin_recv_sem,
):
    chunks = 2 * slabs
    group = lax.axis_index("outer")
    inner = lax.axis_index("inner")
    place = inner % 8
    base = inner - place
    slab = group * slabs_per_group + inner // 8
    x = place // 2
    core = place % 2
    is_back = x // 2
    unit = jnp.where(is_back == 1, 3 - x, x)
    chunk = jnp.where(is_back == 1, chunks - 1 - slab, slab)

    def in_slab(place_to):
        return (group, base + place_to)

    def holder(chunk_to):
        back = chunk_to // slabs
        slab_to = jnp.where(back == 1, chunks - 1 - chunk_to, chunk_to)
        x_to = jnp.where(back == 1, 3 - unit, unit)
        return (
            slab_to // slabs_per_group,
            (slab_to % slabs_per_group) * 8 + x_to * 2 + core,
        )

    def block_of(place_of, back):
        return jnp.where(back == 1, 7 - place_of, place_of)

    def rows_of(block):
        return pl.ds(pl.multiple_of(block * SPAN, SPAN), SPAN)

    sibling = place + 1 - 2 * core
    partner = (3 - x) * 2 + core
    mate = (x + 1 - 2 * (x % 2)) * 2 + core
    far = (3 - (x + 1 - 2 * (x % 2))) * 2 + core
    own_block = block_of(place, is_back)
    own_rows = pl.ds(pl.multiple_of(is_back * SPAN, SPAN), SPAN)
    other_rows = pl.ds(pl.multiple_of((1 - is_back) * SPAN, SPAN), SPAN)

    locals_ = [
        pltpu.make_async_copy(k_hbm.at[own_rows], kv.at[0, 0, 0], local_sem.at[0]),
        pltpu.make_async_copy(v_hbm.at[own_rows], kv.at[0, 0, 1], local_sem.at[1]),
        pltpu.make_async_copy(k_hbm.at[other_rows], kv_other.at[0], local_sem.at[2]),
        pltpu.make_async_copy(v_hbm.at[other_rows], kv_other.at[1], local_sem.at[3]),
        pltpu.make_async_copy(q_hbm.at[other_rows], qd_other.at[0], local_sem.at[4]),
        pltpu.make_async_copy(g_hbm.at[other_rows], qd_other.at[1], local_sem.at[5]),
        pltpu.make_async_copy(q_hbm.at[own_rows], qd.at[0, rows_of(own_block)], local_sem.at[6]),
        pltpu.make_async_copy(g_hbm.at[own_rows], qd.at[1, rows_of(own_block)], local_sem.at[7]),
    ]
    for copy in locals_:
        copy.start()
    seg_copy = pltpu.make_async_copy(seg_hbm, seg, seg_sem)
    seg_copy.start()

    barrier = pltpu.get_barrier_semaphore()
    for step in range(1, 8):
        pl.semaphore_signal(
            barrier, inc=1, device_id=in_slab((place + step) % 8), device_id_type=MESH
        )
    for k in range(1, WINDOW):
        for to, there in ((chunk + k, chunk + k < chunks), (chunk - k, chunk - k >= 0)):

            @pl.when(there)
            def _():
                pl.semaphore_signal(barrier, inc=1, device_id=holder(to), device_id_type=MESH)

    later = jnp.minimum(chunks - 1 - chunk, WINDOW - 1)
    earlier = jnp.minimum(chunk, WINDOW - 1)
    for copy in locals_:
        copy.wait()
    pl.semaphore_wait(barrier, 7 + later + earlier)

    def send(src, dst, send_sem, recv_sem, to):
        copy = pltpu.make_async_remote_copy(
            src_ref=src,
            dst_ref=dst,
            send_sem=send_sem,
            recv_sem=recv_sem,
            device_id=to,
            device_id_type=MESH,
        )
        copy.start()
        return copy

    def arrived(dst, recv_sem):
        pltpu.make_async_copy(dst, dst, recv_sem).wait()

    def qd_block(block):
        return qd.at[:, rows_of(block)]

    def send_block(src, block, sem, to):
        return send(src, qd_block(block), qd_send_sem.at[sem], qd_recv_sem.at[block], in_slab(to))

    sent = []
    sent.append(send(kv_other, kv.at[0, 1], swap_send_sem, swap_recv_sem, in_slab(partner)))

    def kv_copy(k, half):
        return pltpu.make_async_remote_copy(
            src_ref=kv.at[0, half],
            dst_ref=kv.at[k, half],
            send_sem=kv_send_sem.at[k, half],
            recv_sem=kv_recv_sem.at[k, half],
            device_id=holder(chunk + k),
            device_id_type=MESH,
        )

    def kv_start(half):
        for k in range(1, WINDOW):

            @pl.when(chunk + k < chunks)
            def _():
                kv_copy(k, half).start()

    other_block = block_of(place, 1 - is_back)
    sent.append(send_block(qd_other, other_block, 0, far))
    sent.append(send_block(qd_block(own_block), own_block, 1, mate))
    sent.append(send_block(qd_other, other_block, 2, partner))
    kv_start(0)
    sent.append(send_block(qd_block(own_block), own_block, 3, sibling))

    for k in range(1, WINDOW):

        @pl.when(chunk - k < 0)
        def _():
            kv[k] = jnp.zeros(kv.shape[1:], bf16)

    seg_copy.wait()
    doc_ids = lax.broadcasted_iota(jnp.int32, (docs, 128), 0)

    def count(i, acc):
        rows = seg[pl.ds(pl.multiple_of(i * 8, 8), 8), :]
        for r in range(8):
            acc = acc + jnp.where(rows[r : r + 1, :] < doc_ids, 1.0, 0.0)
        return acc

    tally = lax.fori_loop(0, seg.shape[0] // 8, count, jnp.zeros((docs, 128), f32))
    firsts = jnp.sum(tally, axis=1, keepdims=True)
    query_pos = (lax.broadcasted_iota(jnp.int32, (1, CHUNK), 1) + chunk * CHUNK).astype(f32)
    starts = jnp.max(jnp.where(firsts <= query_pos, firsts, 0.0), axis=0, keepdims=True)
    row_ids = lax.broadcasted_iota(jnp.int32, (SPAN, QTILE), 0)
    for k in range(WINDOW):
        key_chunk = chunk - k
        back = (key_chunk + slabs) // slabs - 1
        for half in range(2):
            front_place = jnp.where(half == 0, unit, 3 - unit) * 2 + core
            back_place = jnp.where(half == 0, 3 - unit, unit) * 2 + core
            block = jnp.where(back == 1, 7 - back_place, front_place)
            key_pos = (row_ids + (key_chunk * CHUNK + block * SPAN)).astype(f32)
            for part in range(CHUNK // QTILE):
                lanes = slice(part * QTILE, (part + 1) * QTILE)
                allowed = (key_pos >= starts[:, lanes]) & (key_pos <= query_pos[:, lanes])
                at = (2 * k + half) * SPAN
                bias[part, at : at + SPAN, :] = jnp.where(allowed, 0.0, NEGATIVE)

    arrived(kv.at[0, 1], swap_recv_sem)
    kv_start(1)
    for sem, source in ((4, mate), (5, partner), (6, far)):
        block = block_of(source, is_back)
        arrived(qd_block(block), qd_recv_sem.at[block])
        sent.append(send_block(qd_block(block), block, sem, sibling))
    for step in range(4):
        block = block_of((sibling + 2 * step) % 8, is_back)
        arrived(qd_block(block), qd_recv_sem.at[block])
    for k in range(1, WINDOW):

        @pl.when(chunk - k >= 0)
        def _():
            for half in range(2):
                arrived(kv.at[k, half], kv_recv_sem.at[k, half])

    def tile(n):
        head = n // 2
        part = n % 2
        return (
            part,
            pl.ds(pl.multiple_of(part * QTILE, QTILE), QTILE),
            pl.ds(pl.multiple_of(head * HD, HD), HD),
        )

    def keys_of(k):
        return kv[k, :, 0].reshape(2 * SPAN, HD)

    def values_of(k):
        return kv[k, :, 1].reshape(2 * SPAN, HD)

    shard = 2 * unit + core

    def forward(n, carry):
        part, rows, lanes = tile(n)
        q = qd[0, rows, lanes]
        g = qd[1, rows, lanes]
        top = jnp.full((1, QTILE), NEGATIVE, f32)
        for k in range(WINDOW):
            at = slice(2 * SPAN * k, 2 * SPAN * (k + 1))
            s = dot(keys_of(k), q, ((1,), (1,))) + bias[part, at, :]
            e_buf[n, at, :] = s
            top = jnp.maximum(top, jnp.max(s, axis=0, keepdims=True))
        total = jnp.zeros((1, QTILE), f32)
        slope = jnp.zeros((1, QTILE), f32)
        for k in range(WINDOW):
            at = slice(2 * SPAN * k, 2 * SPAN * (k + 1))
            dp = dot(values_of(k), g, ((1,), (1,)))
            e = jnp.exp2((e_buf[n, at, :] - top) * KAPPA)
            e_buf[n, at, :] = e
            dp_buf[n, at, :] = dp
            total = total + jnp.sum(e, axis=0, keepdims=True)
            slope = slope + jnp.sum(e * dp, axis=0, keepdims=True)
        stat[shard, n, 0:1, :] = top
        stat[shard, n, 1:2, :] = total
        stat[shard, n, 2:3, :] = slope
        return carry

    stat[shard] = jnp.zeros(stat.shape[1:], f32)
    lax.fori_loop(0, QSTEPS, forward, 0)

    for sem, to in ((0, mate), (1, sibling), (2, mate + 1 - 2 * core)):
        sent.append(
            send(
                stat.at[shard],
                stat.at[shard],
                stat_send_sem.at[sem],
                stat_recv_sem.at[shard],
                in_slab(to),
            )
        )
    for step in range(1, 4):
        peer = (shard + step) % 4
        arrived(stat.at[peer], stat_recv_sem.at[peer])

    tops = stat[:, :, 0:1, :]
    top = jnp.max(tops, axis=0)
    factors = jnp.exp2((tops - top[None]) * KAPPA)
    total = jnp.sum(stat[:, :, 1:2, :] * factors, axis=0)
    delta = jnp.sum(stat[:, :, 2:3, :] * factors, axis=0) / total
    ratio = jnp.exp2((stat[shard, :, 0:1, :] - top) * KAPPA) / total

    def dkv_copy(k):
        return pltpu.make_async_remote_copy(
            src_ref=dkv_send.at[k],
            dst_ref=dkv_recv.at[k],
            send_sem=dkv_send_sem.at[k],
            recv_sem=dkv_recv_sem.at[k],
            device_id=holder(chunk - k),
            device_id_type=MESH,
        )

    for k in (4, 3, 2, 1, 0):
        at = slice(2 * SPAN * k, 2 * SPAN * (k + 1))
        dk = jnp.zeros((2 * SPAN, HD), f32)
        dv = jnp.zeros((2 * SPAN, HD), f32)
        for n in range(QSTEPS):
            head, part = n // 2, n % 2
            rows = slice(part * QTILE, (part + 1) * QTILE)
            lanes = slice(head * HD, (head + 1) * HD)
            p = e_buf[n, at, :] * ratio[n]
            ds = (p * (dp_buf[n, at, :] - delta[n])).astype(bf16)
            ds_buf[n, at, :] = ds
            dv = dv + dot(p.astype(bf16), qd[1, rows, lanes], ((1,), (0,)))
            dk = dk + dot(ds, qd[0, rows, lanes], ((1,), (0,)))
        dk = dk * SCALE
        if k == 0:
            dkv_own[:, 0] = dk.reshape(2, SPAN, HD)
            dkv_own[:, 1] = dv.reshape(2, SPAN, HD)
        else:
            dkv_send[k, :, 0] = dk.astype(bf16).reshape(2, SPAN, HD)
            dkv_send[k, :, 1] = dv.astype(bf16).reshape(2, SPAN, HD)

            @pl.when(chunk - k >= 0)
            def _():
                dkv_copy(k).start()

    keys = kv[:, :, 0].reshape(2 * SPAN * WINDOW, HD)
    for n in range(QSTEPS):
        head, part = n // 2, n % 2
        dqt = dot(keys, ds_buf[n], ((0,), (0,)))
        dq_send[part * QTILE : (part + 1) * QTILE, head * HD : (head + 1) * HD] = (
            dqt.T * SCALE
        ).astype(bf16)
    for step in (4, 2, 6, 3, 5, 7, 1):
        to = (place + step) % 8
        sent.append(
            send(
                dq_send.at[rows_of(block_of(to, is_back))],
                dq_recv.at[is_back, shard],
                dq_send_sem.at[step],
                dq_recv_sem.at[is_back, shard],
                in_slab(to),
            )
        )
    dq_recv[is_back, shard] = dq_send[rows_of(own_block), :]

    for k in range(1, WINDOW):

        @pl.when(chunk + k < chunks)
        def _():
            arrived(dkv_recv.at[k], dkv_recv_sem.at[k])
            dkv_own[...] = dkv_own[...] + dkv_recv[k].astype(f32)

    fin_send[...] = dkv_own[1].astype(bf16)
    sent.append(send(fin_send, fin_recv, fin_send_sem, fin_recv_sem, in_slab(partner)))
    dk_out[own_rows, :] = dkv_own[0, 0].astype(bf16)
    dv_out[own_rows, :] = dkv_own[0, 1].astype(bf16)

    for step in range(1, 8):
        source = (place + step) % 8
        source_x = source // 2
        source_back = source_x // 2
        source_unit = jnp.where(source_back == 1, 3 - source_x, source_x)
        source_shard = 2 * source_unit + source % 2
        arrived(
            dq_recv.at[source_back, source_shard], dq_recv_sem.at[source_back, source_shard]
        )
    for back in range(2):
        total_dq = dq_recv[back, 0].astype(f32)
        for j in range(1, 4):
            total_dq = total_dq + dq_recv[back, j].astype(f32)
        dq_out[back * SPAN : (back + 1) * SPAN, :] = total_dq.astype(bf16)
    arrived(fin_recv, fin_recv_sem)
    dk_out[other_rows, :] = fin_recv[0]
    dv_out[other_rows, :] = fin_recv[1]

    for copy in sent:
        copy.wait_send()
    for k in range(1, WINDOW):

        @pl.when(chunk + k < chunks)
        def _():
            for half in range(2):
                kv_copy(k, half).wait_send()

        @pl.when(chunk - k >= 0)
        def _():
            dkv_copy(k).wait_send()


def local(queries, key_rows, value_rows, grad_output, segments):
    groups = lax.axis_size("outer")
    slabs_per_group = lax.axis_size("inner") // 8
    slabs = groups * slabs_per_group
    rows = queries.shape[0]
    positions = segments.shape[0]
    vmem = pltpu.VMEM
    sem = pltpu.SemaphoreType.DMA
    keys = 2 * SPAN * WINDOW
    return pl.pallas_call(
        functools.partial(kernel, slabs_per_group, slabs, 32),
        out_shape=(
            jax.ShapeDtypeStruct((rows, HEADS * HD), bf16),
            jax.ShapeDtypeStruct((rows, HD), bf16),
            jax.ShapeDtypeStruct((rows, HD), bf16),
        ),
        in_specs=[pl.BlockSpec(memory_space=pl.ANY)] * 5,
        out_specs=[pl.BlockSpec(memory_space=pltpu.VMEM)] * 3,
        scratch_shapes=[
            vmem((2, CHUNK, HEADS * HD), bf16),
            vmem((2, SPAN, HEADS * HD), bf16),
            vmem((WINDOW, 2, 2, SPAN, HD), bf16),
            vmem((2, SPAN, HD), bf16),
            vmem((positions // 128, 128), jnp.int32),
            vmem((CHUNK // QTILE, keys, QTILE), f32),
            vmem((QSTEPS, keys, QTILE), f32),
            vmem((QSTEPS, keys, QTILE), f32),
            vmem((QSTEPS, keys, QTILE), bf16),
            vmem((4, QSTEPS, 8, QTILE), f32),
            vmem((CHUNK, HEADS * HD), bf16),
            vmem((2, 4, SPAN, HEADS * HD), bf16),
            vmem((2, 2, SPAN, HD), f32),
            vmem((WINDOW, 2, 2, SPAN, HD), bf16),
            vmem((WINDOW, 2, 2, SPAN, HD), bf16),
            vmem((2, SPAN, HD), bf16),
            vmem((2, SPAN, HD), bf16),
            sem((8,)),
            sem,
            sem((7,)),
            sem((8,)),
            sem,
            sem,
            sem((WINDOW, 2)),
            sem((WINDOW, 2)),
            sem((3,)),
            sem((4,)),
            sem((8,)),
            sem((2, 4)),
            sem((WINDOW,)),
            sem((WINDOW,)),
            sem,
            sem,
        ],
        compiler_params=pltpu.CompilerParams(
            collective_id=0, has_side_effects=True, vmem_limit_bytes=40 * 1024 * 1024
        ),
        name="windowed_backward",
    )(queries, key_rows, value_rows, grad_output, segments.reshape(positions // 128, 128))


def solution(mesh):
    placed = P(("outer", "inner"), None)
    return jax.shard_map(
        local,
        mesh=mesh,
        in_specs=(placed, placed, placed, placed, P()),
        out_specs=(placed, placed, placed),
        check_vma=False,
    )
```

time: 567 us -> 46.9 us (0.08)
  the two profiles are of different devices: /device:TPU:8 before, /device:TPU:28 now
where the time goes in v1:
time: 46.9 us; the launch traced here: 46.6 us
  Pallas kernels  39.9 us (85%)
  local copies, waits for them, and re-layouts  6.07 us (13%)
  between operations  0.65 us (1%)
    pallas_call x1, Pallas kernels, local(): pl.pallas_call(functools.partial(kernel, slabs_per_group, slabs, 32), out...  39.9 us
    unnamed x13, local copies, waits for them, and re-layouts  6.07 us

profile of v1, /device:TPU:28, one launch (start us, length us, event | category | flops | bytes accessed | tf_op | source)
XLA Modules:
  0.0 46.6 jit_solution(5005998411098297383)
XLA Ops:
  0.6 0.0 copy-start
  0.6 0.9 %copy-done = s32[32768]{0:T(1024)S(1)} copy-done((s32[32768]{0:T(1024)S(1)}, s32[32768]{0:T(1024)}, u32[]{:S(2)}) %copy-start) | copy-done | bytes 131096
  1.5 0.0 copy-start.1
  1.5 0.9 %copy-done.1 = bf16[128,384]{1,0:T(8,128)(2,1)S(1)} copy-done((bf16[128,384]{1,0:T(8,128)(2,1)S(1)}, bf16[128,384]{1,0:T(8,128)(2,1)}, u32[]{:S(2)}) %copy-start.1) | copy-done | bytes 98328
  2.4 0.0 copy-start.2
  2.4 0.9 %copy-done.2 = bf16[128,384]{1,0:T(8,128)(2,1)S(1)} copy-done((bf16[128,384]{1,0:T(8,128)(2,1)S(1)}, bf16[128,384]{1,0:T(8,128)(2,1)}, u32[]{:S(2)}) %copy-start.2) | copy-done | bytes 98328
  3.3 0.0 copy-start.3
  3.3 0.8 %copy-done.3 = bf16[128,128]{1,0:T(8,128)(2,1)S(1)} copy-done((bf16[128,128]{1,0:T(8,128)(2,1)S(1)}, bf16[128,128]{1,0:T(8,128)(2,1)}, u32[]{:S(2)}) %copy-start.3) | copy-done | bytes 32792
  4.1 0.0 copy-start.4
  4.1 0.8 %copy-done.4 = bf16[128,128]{1,0:T(8,128)(2,1)S(1)} copy-done((bf16[128,128]{1,0:T(8,128)(2,1)S(1)}, bf16[128,128]{1,0:T(8,128)(2,1)}, u32[]{:S(2)}) %copy-start.4) | copy-done | bytes 32792
  4.8 39.9 %windowed_backward.1 = (bf16[128,384]{1,0:T(8,128)(2,1)S(1)}, bf16[128,128]{1,0:T(8,128)(2,1)S(1)}, bf16[128,128]{1,0:T(8,128)(2,1)S(1)}) custom-call(bf16[128,384]{1,0:T(8,128)(2,1)S(1)} %copy-done.1, bf16[128,128]{1,0:T(8,128)(2,1)S(1)} %copy-done.3, bf16[128,128]{1,0:T(8,128)(2,1)S(1)} %copy-done.4, bf16[128,384]{1,0:T(8,128)(2,1)S(1)} %copy-done.2, ...), custom_call_target="tpu_custom_call" | custom-call | tf_op jit(solution)/shard_map/windowed_backward/pallas_call | solution.py:419
  44.7 0.6 %copy.11 = bf16[128,384]{1,0:T(8,128)(2,1)} copy(bf16[128,384]{1,0:T(8,128)(2,1)S(1)} %get-tuple-element.6) | data formatting | bytes 196608
  45.4 0.6 %copy.12 = bf16[128,128]{1,0:T(8,128)(2,1)} copy(bf16[128,128]{1,0:T(8,128)(2,1)S(1)} %get-tuple-element.7) | data formatting | bytes 65536
  46.0 0.6 %copy.13 = bf16[128,128]{1,0:T(8,128)(2,1)} copy(bf16[128,128]{1,0:T(8,128)(2,1)S(1)} %get-tuple-element.8) | data formatting | bytes 65536
Async XLA Ops:
  0.6 0.9 %copy-start = (s32[32768]{0:T(1024)S(1)}, s32[32768]{0:T(1024)}, u32[]{:S(2)}) copy-start(s32[32768]{0:T(1024)} %param.9) | copy-start | bytes 393220
  1.5 0.9 %copy-start.1 = (bf16[128,384]{1,0:T(8,128)(2,1)S(1)}, bf16[128,384]{1,0:T(8,128)(2,1)}, u32[]{:S(2)}) copy-start(bf16[128,384]{1,0:T(8,128)(2,1)} %q_hbm.1) | copy-start | bytes 294916
  2.4 0.9 %copy-start.2 = (bf16[128,384]{1,0:T(8,128)(2,1)S(1)}, bf16[128,384]{1,0:T(8,128)(2,1)}, u32[]{:S(2)}) copy-start(bf16[128,384]{1,0:T(8,128)(2,1)} %g_hbm.1) | copy-start | bytes 294916
  3.3 0.8 %copy-start.3 = (bf16[128,128]{1,0:T(8,128)(2,1)S(1)}, bf16[128,128]{1,0:T(8,128)(2,1)}, u32[]{:S(2)}) copy-start(bf16[128,128]{1,0:T(8,128)(2,1)} %k_hbm.1) | copy-start | bytes 98308
  4.1 0.8 %copy-start.4 = (bf16[128,128]{1,0:T(8,128)(2,1)S(1)}, bf16[128,128]{1,0:T(8,128)(2,1)}, u32[]{:S(2)}) copy-start(bf16[128,128]{1,0:T(8,128)(2,1)} %v_hbm.1) | copy-start | bytes 98308

commit v2 on v1

--- a/solution.py
+++ b/solution.py
@@ -10,6 +10,7 @@
 
 MESH = pl.DeviceIdType.MESH
 NEGATIVE = -1e30
+TINY = 1e-30
 HD = 128
 HEADS = 3
 SPAN = 64
@@ -54,8 +55,6 @@
     dkv_own,
     dkv_send,
     dkv_recv,
-    fin_send,
-    fin_recv,
     local_sem,
     seg_sem,
     qd_send_sem,
@@ -70,8 +69,6 @@
     dq_recv_sem,
     dkv_send_sem,
     dkv_recv_sem,
-    fin_send_sem,
-    fin_recv_sem,
 ):
     chunks = 2 * slabs
     group = lax.axis_index("outer")
@@ -84,14 +81,15 @@
     is_back = x // 2
     unit = jnp.where(is_back == 1, 3 - x, x)
     chunk = jnp.where(is_back == 1, chunks - 1 - slab, slab)
+    other_chunk = chunks - 1 - chunk
 
     def in_slab(place_to):
         return (group, base + place_to)
 
-    def holder(chunk_to):
+    def holder(chunk_to, half=0):
         back = chunk_to // slabs
         slab_to = jnp.where(back == 1, chunks - 1 - chunk_to, chunk_to)
-        x_to = jnp.where(back == 1, 3 - unit, unit)
+        x_to = jnp.where((back + half) % 2 == 1, 3 - unit, unit)
         return (
             slab_to // slabs_per_group,
             (slab_to % slabs_per_group) * 8 + x_to * 2 + core,
@@ -132,17 +130,26 @@
             barrier, inc=1, device_id=in_slab((place + step) % 8), device_id_type=MESH
         )
     for k in range(1, WINDOW):
-        for to, there in ((chunk + k, chunk + k < chunks), (chunk - k, chunk - k >= 0)):
+        for to, half, there in (
+            (chunk + k, 0, chunk + k < chunks),
+            (chunk - k, 0, chunk - k >= 0),
+            (other_chunk + k, 0, (other_chunk + k < chunks) & (other_chunk + k != chunk)),
+            (chunk - k, 1, (chunk - k >= 0) & (chunk - k != other_chunk)),
+        ):
 
             @pl.when(there)
             def _():
-                pl.semaphore_signal(barrier, inc=1, device_id=holder(to), device_id_type=MESH)
+                pl.semaphore_signal(
+                    barrier, inc=1, device_id=holder(to, half), device_id_type=MESH
+                )
 
     later = jnp.minimum(chunks - 1 - chunk, WINDOW - 1)
     earlier = jnp.minimum(chunk, WINDOW - 1)
+    apart = chunk - other_chunk
+    own_second = jnp.where((apart > 0) & (apart < WINDOW), 1, 0)
     for copy in locals_:
         copy.wait()
-    pl.semaphore_wait(barrier, 7 + later + earlier)
+    pl.semaphore_wait(barrier, 7 + later + 3 * earlier - 2 * own_second)
 
     def send(src, dst, send_sem, recv_sem, to):
         copy = pltpu.make_async_remote_copy(
@@ -279,9 +286,9 @@
             dp_buf[n, at, :] = dp
             total = total + jnp.sum(e, axis=0, keepdims=True)
             slope = slope + jnp.sum(e * dp, axis=0, keepdims=True)
-        stat[shard, n, 0:1, :] = top
-        stat[shard, n, 1:2, :] = total
-        stat[shard, n, 2:3, :] = slope
+        stat[shard, 0, pl.ds(n, 1), :] = top
+        stat[shard, 1, pl.ds(n, 1), :] = total
+        stat[shard, 2, pl.ds(n, 1), :] = slope
         return carry
 
     stat[shard] = jnp.zeros(stat.shape[1:], f32)
@@ -301,20 +308,20 @@
         peer = (shard + step) % 4
         arrived(stat.at[peer], stat_recv_sem.at[peer])
 
-    tops = stat[:, :, 0:1, :]
+    tops = stat[:, 0]
     top = jnp.max(tops, axis=0)
     factors = jnp.exp2((tops - top[None]) * KAPPA)
-    total = jnp.sum(stat[:, :, 1:2, :] * factors, axis=0)
-    delta = jnp.sum(stat[:, :, 2:3, :] * factors, axis=0) / total
-    ratio = jnp.exp2((stat[shard, :, 0:1, :] - top) * KAPPA) / total
-
-    def dkv_copy(k):
+    inverse = 1.0 / jnp.maximum(jnp.sum(stat[:, 1] * factors, axis=0), TINY)
+    delta = jnp.sum(stat[:, 2] * factors, axis=0) * inverse
+    ratio = jnp.exp2((stat[shard, 0] - top) * KAPPA) * inverse
+
+    def dkv_copy(k, half):
         return pltpu.make_async_remote_copy(
-            src_ref=dkv_send.at[k],
-            dst_ref=dkv_recv.at[k],
-            send_sem=dkv_send_sem.at[k],
-            recv_sem=dkv_recv_sem.at[k],
-            device_id=holder(chunk - k),
+            src_ref=dkv_send.at[k, half],
+            dst_ref=dkv_recv.at[half, k],
+            send_sem=dkv_send_sem.at[half, k],
+            recv_sem=dkv_recv_sem.at[half, k],
+            device_id=holder(chunk - k, half),
             device_id_type=MESH,
         )
 
@@ -326,22 +333,41 @@
             head, part = n // 2, n % 2
             rows = slice(part * QTILE, (part + 1) * QTILE)
             lanes = slice(head * HD, (head + 1) * HD)
-            p = e_buf[n, at, :] * ratio[n]
-            ds = (p * (dp_buf[n, at, :] - delta[n])).astype(bf16)
+            p = e_buf[n, at, :] * ratio[n : n + 1]
+            ds = (p * (dp_buf[n, at, :] - delta[n : n + 1])).astype(bf16)
             ds_buf[n, at, :] = ds
             dv = dv + dot(p.astype(bf16), qd[1, rows, lanes], ((1,), (0,)))
             dk = dk + dot(ds, qd[0, rows, lanes], ((1,), (0,)))
         dk = dk * SCALE
         if k == 0:
-            dkv_own[:, 0] = dk.reshape(2, SPAN, HD)
-            dkv_own[:, 1] = dv.reshape(2, SPAN, HD)
+            dkv_own[0] = dk[:SPAN]
+            dkv_own[1] = dv[:SPAN]
+            dkv_send[0, 1, 0] = dk[SPAN:].astype(bf16)
+            dkv_send[0, 1, 1] = dv[SPAN:].astype(bf16)
+            sent.append(
+                send(
+                    dkv_send.at[0, 1],
+                    dkv_recv.at[1, 0],
+                    dkv_send_sem.at[1, 0],
+                    dkv_recv_sem.at[1, 0],
+                    in_slab(partner),
+                )
+            )
         else:
             dkv_send[k, :, 0] = dk.astype(bf16).reshape(2, SPAN, HD)
             dkv_send[k, :, 1] = dv.astype(bf16).reshape(2, SPAN, HD)
 
             @pl.when(chunk - k >= 0)
             def _():
-                dkv_copy(k).start()
+                dkv_copy(k, 0).start()
+
+            @pl.when((chunk - k >= 0) & (apart != k))
+            def _():
+                dkv_copy(k, 1).start()
+
+            @pl.when(apart == k)
+            def _():
+                dkv_recv[1, k] = dkv_send[k, 1]
 
     keys = kv[:, :, 0].reshape(2 * SPAN * WINDOW, HD)
     for n in range(QSTEPS):
@@ -363,17 +389,25 @@
         )
     dq_recv[is_back, shard] = dq_send[rows_of(own_block), :]
 
-    for k in range(1, WINDOW):
-
-        @pl.when(chunk + k < chunks)
-        def _():
-            arrived(dkv_recv.at[k], dkv_recv_sem.at[k])
-            dkv_own[...] = dkv_own[...] + dkv_recv[k].astype(f32)
-
-    fin_send[...] = dkv_own[1].astype(bf16)
-    sent.append(send(fin_send, fin_recv, fin_send_sem, fin_recv_sem, in_slab(partner)))
-    dk_out[own_rows, :] = dkv_own[0, 0].astype(bf16)
-    dv_out[own_rows, :] = dkv_own[0, 1].astype(bf16)
+    def add_arrived(half, there, k, total):
+        @pl.when(there & (apart != k) if half == 1 else there)
+        def _():
+            arrived(dkv_recv.at[half, k], dkv_recv_sem.at[half, k])
+
+        @pl.when(there)
+        def _():
+            total[...] = total[...] + dkv_recv[half, k].astype(f32)
+
+    for k in range(4, 0, -1):
+        add_arrived(0, chunk + k < chunks, k, dkv_own)
+    dk_out[own_rows, :] = dkv_own[0].astype(bf16)
+    dv_out[own_rows, :] = dkv_own[1].astype(bf16)
+    arrived(dkv_recv.at[1, 0], dkv_recv_sem.at[1, 0])
+    dkv_own[...] = dkv_recv[1, 0].astype(f32)
+    for k in range(4, 0, -1):
+        add_arrived(1, other_chunk + k < chunks, k, dkv_own)
+    dk_out[other_rows, :] = dkv_own[0].astype(bf16)
+    dv_out[other_rows, :] = dkv_own[1].astype(bf16)
 
     for step in range(1, 8):
         source = (place + step) % 8
@@ -389,9 +423,6 @@
         for j in range(1, 4):
             total_dq = total_dq + dq_recv[back, j].astype(f32)
         dq_out[back * SPAN : (back + 1) * SPAN, :] = total_dq.astype(bf16)
-    arrived(fin_recv, fin_recv_sem)
-    dk_out[other_rows, :] = fin_recv[0]
-    dv_out[other_rows, :] = fin_recv[1]
 
     for copy in sent:
         copy.wait_send()
@@ -404,7 +435,22 @@
 
         @pl.when(chunk - k >= 0)
         def _():
-            dkv_copy(k).wait_send()
+            dkv_copy(k, 0).wait_send()
+
+        @pl.when((chunk - k >= 0) & (apart != k))
+        def _():
+            dkv_copy(k, 1).wait_send()
+
+
+def write_out(dq, dk, dv, dq_out, dk_out, dv_out, sems):
+    copies = [
+        pltpu.make_async_copy(src, dst, sems.at[i])
+        for i, (src, dst) in enumerate(((dq, dq_out), (dk, dk_out), (dv, dv_out)))
+    ]
+    for copy in copies:
+        copy.start()
+    for copy in copies:
+        copy.wait()
 
 
 def local(queries, key_rows, value_rows, grad_output, segments):
@@ -416,13 +462,14 @@
     vmem = pltpu.VMEM
     sem = pltpu.SemaphoreType.DMA
     keys = 2 * SPAN * WINDOW
-    return pl.pallas_call(
+    shapes = (
+        jax.ShapeDtypeStruct((rows, HEADS * HD), bf16),
+        jax.ShapeDtypeStruct((rows, HD), bf16),
+        jax.ShapeDtypeStruct((rows, HD), bf16),
+    )
+    grads = pl.pallas_call(
         functools.partial(kernel, slabs_per_group, slabs, 32),
-        out_shape=(
-            jax.ShapeDtypeStruct((rows, HEADS * HD), bf16),
-            jax.ShapeDtypeStruct((rows, HD), bf16),
-            jax.ShapeDtypeStruct((rows, HD), bf16),
-        ),
+        out_shape=shapes,
         in_specs=[pl.BlockSpec(memory_space=pl.ANY)] * 5,
         out_specs=[pl.BlockSpec(memory_space=pltpu.VMEM)] * 3,
         scratch_shapes=[
@@ -435,14 +482,12 @@
             vmem((QSTEPS, keys, QTILE), f32),
             vmem((QSTEPS, keys, QTILE), f32),
             vmem((QSTEPS, keys, QTILE), bf16),
-            vmem((4, QSTEPS, 8, QTILE), f32),
+            vmem((4, 3, 8, QTILE), f32),
             vmem((CHUNK, HEADS * HD), bf16),
             vmem((2, 4, SPAN, HEADS * HD), bf16),
-            vmem((2, 2, SPAN, HD), f32),
+            vmem((2, SPAN, HD), f32),
             vmem((WINDOW, 2, 2, SPAN, HD), bf16),
-            vmem((WINDOW, 2, 2, SPAN, HD), bf16),
-            vmem((2, SPAN, HD), bf16),
-            vmem((2, SPAN, HD), bf16),
+            vmem((2, WINDOW, 2, SPAN, HD), bf16),
             sem((8,)),
             sem,
             sem((7,)),
@@ -455,16 +500,22 @@
             sem((4,)),
             sem((8,)),
             sem((2, 4)),
-            sem((WINDOW,)),
-            sem((WINDOW,)),
-            sem,
-            sem,
+            sem((2, WINDOW)),
+            sem((2, WINDOW)),
         ],
         compiler_params=pltpu.CompilerParams(
-            collective_id=0, has_side_effects=True, vmem_limit_bytes=40 * 1024 * 1024
+            collective_id=0, has_side_effects=True, vmem_limit_bytes=60 * 1024 * 1024
         ),
         name="windowed_backward",
     )(queries, key_rows, value_rows, grad_output, segments.reshape(positions // 128, 128))
+    return pl.pallas_call(
+        write_out,
+        out_shape=shapes,
+        in_specs=[pl.BlockSpec(memory_space=pltpu.VMEM)] * 3,
+        out_specs=[pl.BlockSpec(memory_space=pl.ANY)] * 3,
+        scratch_shapes=[sem((3,))],
+        name="write_out",
+    )(*grads)
 
 
 def solution(mesh):

time: 46.9 us -> 40.3 us (0.86)
  the two profiles are of different devices: /device:TPU:28 before, /device:TPU:57 now
where the time goes in v2:
time: 40.3 us; the launch traced here: 40.2 us
  Pallas kernels  39.5 us (98%)
  between operations  0.64 us (2%)
    pallas_call x1, Pallas kernels, local(): pl.pallas_call(functools.partial(kernel, slabs_per_group, slabs, 32), out...  37.9 us
    pallas_call x1, Pallas kernels, local(): pl.pallas_call(write_out, out_shape=shapes, in_specs=[pl.BlockSpec(memory...  1.6 us

profile of v2, /device:TPU:57, one launch (start us, length us, event | category | flops | bytes accessed | tf_op | source)
XLA Modules:
  0.0 40.2 jit_solution(14811020783687427790)
XLA Ops:
  0.6 37.9 %windowed_backward.1 = (bf16[128,384]{1,0:T(8,128)(2,1)}, bf16[128,128]{1,0:T(8,128)(2,1)}, bf16[128,128]{1,0:T(8,128)(2,1)}) custom-call(bf16[128,384]{1,0:T(8,128)(2,1)} %q_hbm.1, bf16[128,128]{1,0:T(8,128)(2,1)} %k_hbm.1, bf16[128,128]{1,0:T(8,128)(2,1)} %v_hbm.1, bf16[128,384]{1,0:T(8,128)(2,1)} %g_hbm.1, s32[256,128]{1,0:T(8,128)} %bitcast.1), custom_call_target="tpu_custom_call" | custom-call | tf_op jit(solution)/shard_map/windowed_backward/pallas_call | solution.py:470
  38.6 1.6 %write_out.1 = (bf16[128,384]{1,0:T(8,128)(2,1)}, bf16[128,128]{1,0:T(8,128)(2,1)}, bf16[128,128]{1,0:T(8,128)(2,1)}) custom-call(bf16[128,384]{1,0:T(8,128)(2,1)} %get-tuple-element.6.dq, bf16[128,128]{1,0:T(8,128)(2,1)} %get-tuple-element.7.dk, bf16[128,128]{1,0:T(8,128)(2,1)} %get-tuple-element.8.dv), custom_call_target="tpu_custom_call" | custom-call | tf_op jit(solution)/shard_map/write_out/pallas_call | solution.py:511

commit v3 on v2

--- a/solution.py
+++ b/solution.py
@@ -15,6 +15,7 @@
 HEADS = 3
 SPAN = 64
 CHUNK = 512
+STRAIGHT = ()
 WINDOW = 5
 QTILE = 256
 QSTEPS = HEADS * (CHUNK // QTILE)
@@ -71,6 +72,7 @@
     dkv_recv_sem,
 ):
     chunks = 2 * slabs
+    sent = []
     group = lax.axis_index("outer")
     inner = lax.axis_index("inner")
     place = inner % 8
@@ -125,31 +127,23 @@
     seg_copy.start()
 
     barrier = pltpu.get_barrier_semaphore()
+    for k in (2, 3, 1, 4):
+        for to, there in ((chunk + k, chunk + k < chunks), (chunk - k, chunk - k >= 0)):
+
+            @pl.when(there)
+            def _():
+                pl.semaphore_signal(barrier, inc=1, device_id=holder(to), device_id_type=MESH)
+
     for step in range(1, 8):
         pl.semaphore_signal(
             barrier, inc=1, device_id=in_slab((place + step) % 8), device_id_type=MESH
         )
-    for k in range(1, WINDOW):
-        for to, half, there in (
-            (chunk + k, 0, chunk + k < chunks),
-            (chunk - k, 0, chunk - k >= 0),
-            (other_chunk + k, 0, (other_chunk + k < chunks) & (other_chunk + k != chunk)),
-            (chunk - k, 1, (chunk - k >= 0) & (chunk - k != other_chunk)),
-        ):
-
-            @pl.when(there)
-            def _():
-                pl.semaphore_signal(
-                    barrier, inc=1, device_id=holder(to, half), device_id_type=MESH
-                )
-
     later = jnp.minimum(chunks - 1 - chunk, WINDOW - 1)
     earlier = jnp.minimum(chunk, WINDOW - 1)
     apart = chunk - other_chunk
-    own_second = jnp.where((apart > 0) & (apart < WINDOW), 1, 0)
     for copy in locals_:
         copy.wait()
-    pl.semaphore_wait(barrier, 7 + later + 3 * earlier - 2 * own_second)
+    pl.semaphore_wait(barrier, 7 + later + earlier)
 
     def send(src, dst, send_sem, recv_sem, to):
         copy = pltpu.make_async_remote_copy(
@@ -172,31 +166,42 @@
     def send_block(src, block, sem, to):
         return send(src, qd_block(block), qd_send_sem.at[sem], qd_recv_sem.at[block], in_slab(to))
 
-    sent = []
     sent.append(send(kv_other, kv.at[0, 1], swap_send_sem, swap_recv_sem, in_slab(partner)))
 
     def kv_copy(k, half):
+        straight = half == 1 and k in STRAIGHT
         return pltpu.make_async_remote_copy(
-            src_ref=kv.at[0, half],
+            src_ref=kv_other if straight else kv.at[0, half],
             dst_ref=kv.at[k, half],
             send_sem=kv_send_sem.at[k, half],
             recv_sem=kv_recv_sem.at[k, half],
-            device_id=holder(chunk + k),
+            device_id=holder((other_chunk if straight else chunk) + k),
             device_id_type=MESH,
         )
 
-    def kv_start(half):
-        for k in range(1, WINDOW):
-
-            @pl.when(chunk + k < chunks)
+    def kv_sent(k, half):
+        if half == 1 and k in STRAIGHT:
+            return (other_chunk + k < chunks) & (apart != k)
+        return chunk + k < chunks
+
+    def kv_arrives(k, half):
+        if half == 1 and k in STRAIGHT:
+            return (chunk - k >= 0) & (apart != k)
+        return chunk - k >= 0
+
+    def kv_start(half, which):
+        for k in which:
+
+            @pl.when(kv_sent(k, half))
             def _():
                 kv_copy(k, half).start()
 
     other_block = block_of(place, 1 - is_back)
+    kv_start(1, STRAIGHT)
+    kv_start(0, (2, 3, 1, 4))
     sent.append(send_block(qd_other, other_block, 0, far))
     sent.append(send_block(qd_block(own_block), own_block, 1, mate))
     sent.append(send_block(qd_other, other_block, 2, partner))
-    kv_start(0)
     sent.append(send_block(qd_block(own_block), own_block, 3, sibling))
 
     for k in range(1, WINDOW):
@@ -204,6 +209,12 @@
         @pl.when(chunk - k < 0)
         def _():
             kv[k] = jnp.zeros(kv.shape[1:], bf16)
+
+        if k in STRAIGHT:
+
+            @pl.when(apart == k)
+            def _():
+                kv[k, 1] = kv_other[...]
 
     seg_copy.wait()
     doc_ids = lax.broadcasted_iota(jnp.int32, (docs, 128), 0)
@@ -234,7 +245,7 @@
                 bias[part, at : at + SPAN, :] = jnp.where(allowed, 0.0, NEGATIVE)
 
     arrived(kv.at[0, 1], swap_recv_sem)
-    kv_start(1)
+    kv_start(1, [k for k in (2, 3, 1, 4) if k not in STRAIGHT])
     for sem, source in ((4, mate), (5, partner), (6, far)):
         block = block_of(source, is_back)
         arrived(qd_block(block), qd_recv_sem.at[block])
@@ -244,9 +255,10 @@
         arrived(qd_block(block), qd_recv_sem.at[block])
     for k in range(1, WINDOW):
 
-        @pl.when(chunk - k >= 0)
-        def _():
-            for half in range(2):
+        for half in range(2):
+
+            @pl.when(kv_arrives(k, half))
+            def _():
                 arrived(kv.at[k, half], kv_recv_sem.at[k, half])
 
     def tile(n):
@@ -265,7 +277,6 @@
         return kv[k, :, 1].reshape(2 * SPAN, HD)
 
     shard = 2 * unit + core
-
     def forward(n, carry):
         part, rows, lanes = tile(n)
         q = qd[0, rows, lanes]
@@ -293,7 +304,6 @@
 
     stat[shard] = jnp.zeros(stat.shape[1:], f32)
     lax.fori_loop(0, QSTEPS, forward, 0)
-
     for sem, to in ((0, mate), (1, sibling), (2, mate + 1 - 2 * core)):
         sent.append(
             send(
@@ -307,14 +317,12 @@
     for step in range(1, 4):
         peer = (shard + step) % 4
         arrived(stat.at[peer], stat_recv_sem.at[peer])
-
     tops = stat[:, 0]
     top = jnp.max(tops, axis=0)
     factors = jnp.exp2((tops - top[None]) * KAPPA)
     inverse = 1.0 / jnp.maximum(jnp.sum(stat[:, 1] * factors, axis=0), TINY)
     delta = jnp.sum(stat[:, 2] * factors, axis=0) * inverse
     ratio = jnp.exp2((stat[shard, 0] - top) * KAPPA) * inverse
-
     def dkv_copy(k, half):
         return pltpu.make_async_remote_copy(
             src_ref=dkv_send.at[k, half],
@@ -324,8 +332,7 @@
             device_id=holder(chunk - k, half),
             device_id_type=MESH,
         )
-
-    for k in (4, 3, 2, 1, 0):
+    for k in (2, 3, 1, 4, 0):
         at = slice(2 * SPAN * k, 2 * SPAN * (k + 1))
         dk = jnp.zeros((2 * SPAN, HD), f32)
         dv = jnp.zeros((2 * SPAN, HD), f32)
@@ -368,7 +375,6 @@
             @pl.when(apart == k)
             def _():
                 dkv_recv[1, k] = dkv_send[k, 1]
-
     keys = kv[:, :, 0].reshape(2 * SPAN * WINDOW, HD)
     for n in range(QSTEPS):
         head, part = n // 2, n % 2
@@ -388,7 +394,6 @@
             )
         )
     dq_recv[is_back, shard] = dq_send[rows_of(own_block), :]
-
     def add_arrived(half, there, k, total):
         @pl.when(there & (apart != k) if half == 1 else there)
         def _():
@@ -408,7 +413,6 @@
         add_arrived(1, other_chunk + k < chunks, k, dkv_own)
     dk_out[other_rows, :] = dkv_own[0].astype(bf16)
     dv_out[other_rows, :] = dkv_own[1].astype(bf16)
-
     for step in range(1, 8):
         source = (place + step) % 8
         source_x = source // 2
@@ -423,15 +427,16 @@
         for j in range(1, 4):
             total_dq = total_dq + dq_recv[back, j].astype(f32)
         dq_out[back * SPAN : (back + 1) * SPAN, :] = total_dq.astype(bf16)
-
     for copy in sent:
         copy.wait_send()
     for k in range(1, WINDOW):
 
-        @pl.when(chunk + k < chunks)
-        def _():
-            for half in range(2):
+        for half in range(2):
+
+            @pl.when(kv_sent(k, half))
+            def _():
                 kv_copy(k, half).wait_send()
+    for k in range(1, WINDOW):
 
         @pl.when(chunk - k >= 0)
         def _():

time: 40.3 us -> 40.7 us (level)
  the two profiles are of different devices: /device:TPU:57 before, /device:TPU:121 now
where the time goes in v3:
time: 40.7 us; the launch traced here: 40.5 us
  Pallas kernels  39.8 us (98%)
  between operations  0.64 us (2%)
    pallas_call x1, Pallas kernels, local(): pl.pallas_call(functools.partial(kernel, slabs_per_group, slabs, 32), out...  38.2 us
    pallas_call x1, Pallas kernels, local(): pl.pallas_call(write_out, out_shape=shapes, in_specs=[pl.BlockSpec(memory...  1.6 us

profile of v3, /device:TPU:121, one launch (start us, length us, event | category | flops | bytes accessed | tf_op | source)
XLA Modules:
  0.0 40.5 jit_solution(16111858397763276531)
XLA Ops:
  0.6 38.2 %windowed_backward.1 = (bf16[128,384]{1,0:T(8,128)(2,1)}, bf16[128,128]{1,0:T(8,128)(2,1)}, bf16[128,128]{1,0:T(8,128)(2,1)}) custom-call(bf16[128,384]{1,0:T(8,128)(2,1)} %q_hbm.1, bf16[128,128]{1,0:T(8,128)(2,1)} %k_hbm.1, bf16[128,128]{1,0:T(8,128)(2,1)} %v_hbm.1, bf16[128,384]{1,0:T(8,128)(2,1)} %g_hbm.1, s32[256,128]{1,0:T(8,128)} %bitcast.1), custom_call_target="tpu_custom_call" | custom-call | tf_op jit(solution)/shard_map/windowed_backward/pallas_call | solution.py:475
  38.9 1.6 %write_out.1 = (bf16[128,384]{1,0:T(8,128)(2,1)}, bf16[128,128]{1,0:T(8,128)(2,1)}, bf16[128,128]{1,0:T(8,128)(2,1)}) custom-call(bf16[128,384]{1,0:T(8,128)(2,1)} %get-tuple-element.6.dq, bf16[128,128]{1,0:T(8,128)(2,1)} %get-tuple-element.7.dk, bf16[128,128]{1,0:T(8,128)(2,1)} %get-tuple-element.8.dv), custom_call_target="tpu_custom_call" | custom-call | tf_op jit(solution)/shard_map/write_out/pallas_call | solution.py:516

commit v4 on v2

--- a/solution.py
+++ b/solution.py
@@ -46,6 +46,7 @@
     kv_other,
     seg,
     bias,
+    half_stat,
     e_buf,
     dp_buf,
     ds_buf,
@@ -55,6 +56,8 @@
     dkv_own,
     dkv_send,
     dkv_recv,
+    near_sem,
+    far_sem,
     local_sem,
     seg_sem,
     qd_send_sem,
@@ -71,6 +74,7 @@
     dkv_recv_sem,
 ):
     chunks = 2 * slabs
+    sent = []
     group = lax.axis_index("outer")
     inner = lax.axis_index("inner")
     place = inner % 8
@@ -86,13 +90,13 @@
     def in_slab(place_to):
         return (group, base + place_to)
 
-    def holder(chunk_to, half=0):
+    def holder(chunk_to, half=0, core_to=core):
         back = chunk_to // slabs
         slab_to = jnp.where(back == 1, chunks - 1 - chunk_to, chunk_to)
         x_to = jnp.where((back + half) % 2 == 1, 3 - unit, unit)
         return (
             slab_to // slabs_per_group,
-            (slab_to % slabs_per_group) * 8 + x_to * 2 + core,
+            (slab_to % slabs_per_group) * 8 + x_to * 2 + core_to,
         )
 
     def block_of(place_of, back):
@@ -125,31 +129,35 @@
     seg_copy.start()
 
     barrier = pltpu.get_barrier_semaphore()
-    for step in range(1, 8):
-        pl.semaphore_signal(
-            barrier, inc=1, device_id=in_slab((place + step) % 8), device_id_type=MESH
-        )
-    for k in range(1, WINDOW):
-        for to, half, there in (
-            (chunk + k, 0, chunk + k < chunks),
-            (chunk - k, 0, chunk - k >= 0),
-            (other_chunk + k, 0, (other_chunk + k < chunks) & (other_chunk + k != chunk)),
-            (chunk - k, 1, (chunk - k >= 0) & (chunk - k != other_chunk)),
-        ):
-
-            @pl.when(there)
-            def _():
-                pl.semaphore_signal(
-                    barrier, inc=1, device_id=holder(to, half), device_id_type=MESH
-                )
+    for k in (2, 3, 1, 4):
+
+        @pl.when(chunk - k >= 0)
+        def _():
+            pl.semaphore_signal(
+                barrier, inc=1, device_id=holder(chunk - k, 0, 1), device_id_type=MESH
+            )
+
+    for step in range(4):
+        to_x = (x + step) % 4
+
+        @pl.when((step > 0) | (core == 1))
+        def _():
+            pl.semaphore_signal(barrier, inc=1, device_id=in_slab(2 * to_x), device_id_type=MESH)
 
     later = jnp.minimum(chunks - 1 - chunk, WINDOW - 1)
-    earlier = jnp.minimum(chunk, WINDOW - 1)
     apart = chunk - other_chunk
-    own_second = jnp.where((apart > 0) & (apart < WINDOW), 1, 0)
+
+    @pl.when(core == 0)
+    def _():
+        pl.semaphore_wait(barrier, 7)
+        pl.semaphore_signal(near_sem, inc=1, device_id=in_slab(sibling), device_id_type=MESH)
+
+    @pl.when(core == 1)
+    def _():
+        pl.semaphore_wait(near_sem, 1)
+
     for copy in locals_:
         copy.wait()
-    pl.semaphore_wait(barrier, 7 + later + 3 * earlier - 2 * own_second)
 
     def send(src, dst, send_sem, recv_sem, to):
         copy = pltpu.make_async_remote_copy(
@@ -172,21 +180,20 @@
     def send_block(src, block, sem, to):
         return send(src, qd_block(block), qd_send_sem.at[sem], qd_recv_sem.at[block], in_slab(to))
 
-    sent = []
-    sent.append(send(kv_other, kv.at[0, 1], swap_send_sem, swap_recv_sem, in_slab(partner)))
+    sent.append(send(kv_other, kv.at[1, 0], swap_send_sem, swap_recv_sem, in_slab(partner)))
 
     def kv_copy(k, half):
         return pltpu.make_async_remote_copy(
-            src_ref=kv.at[0, half],
-            dst_ref=kv.at[k, half],
-            send_sem=kv_send_sem.at[k, half],
-            recv_sem=kv_recv_sem.at[k, half],
+            src_ref=kv.at[half, 0],
+            dst_ref=kv.at[half, k],
+            send_sem=kv_send_sem.at[half, k],
+            recv_sem=kv_recv_sem.at[half, k],
             device_id=holder(chunk + k),
             device_id_type=MESH,
         )
 
     def kv_start(half):
-        for k in range(1, WINDOW):
+        for k in (2, 3, 1, 4):
 
             @pl.when(chunk + k < chunks)
             def _():
@@ -196,14 +203,29 @@
     sent.append(send_block(qd_other, other_block, 0, far))
     sent.append(send_block(qd_block(own_block), own_block, 1, mate))
     sent.append(send_block(qd_other, other_block, 2, partner))
+    sent.append(send_block(qd_block(own_block), own_block, 3, sibling))
+
+    @pl.when(core == 1)
+    def _():
+        @pl.when(later > 0)
+        def _():
+            pl.semaphore_wait(barrier, 2 * later)
+
+        pl.semaphore_signal(far_sem, inc=1, device_id=in_slab(sibling), device_id_type=MESH)
+
+    @pl.when(core == 0)
+    def _():
+        pl.semaphore_wait(far_sem, 1)
+
     kv_start(0)
-    sent.append(send_block(qd_block(own_block), own_block, 3, sibling))
+    arrived(kv.at[1, 0], swap_recv_sem)
+    kv_start(1)
 
     for k in range(1, WINDOW):
 
         @pl.when(chunk - k < 0)
         def _():
-            kv[k] = jnp.zeros(kv.shape[1:], bf16)
+            kv[:, k] = jnp.zeros((2,) + kv.shape[2:], bf16)
 
     seg_copy.wait()
     doc_ids = lax.broadcasted_iota(jnp.int32, (docs, 128), 0)
@@ -230,11 +252,9 @@
             for part in range(CHUNK // QTILE):
                 lanes = slice(part * QTILE, (part + 1) * QTILE)
                 allowed = (key_pos >= starts[:, lanes]) & (key_pos <= query_pos[:, lanes])
-                at = (2 * k + half) * SPAN
+                at = (WINDOW * half + k) * SPAN
                 bias[part, at : at + SPAN, :] = jnp.where(allowed, 0.0, NEGATIVE)
 
-    arrived(kv.at[0, 1], swap_recv_sem)
-    kv_start(1)
     for sem, source in ((4, mate), (5, partner), (6, far)):
         block = block_of(source, is_back)
         arrived(qd_block(block), qd_recv_sem.at[block])
@@ -242,58 +262,45 @@
     for step in range(4):
         block = block_of((sibling + 2 * step) % 8, is_back)
         arrived(qd_block(block), qd_recv_sem.at[block])
-    for k in range(1, WINDOW):
-
-        @pl.when(chunk - k >= 0)
-        def _():
-            for half in range(2):
-                arrived(kv.at[k, half], kv_recv_sem.at[k, half])
-
-    def tile(n):
-        head = n // 2
-        part = n % 2
-        return (
-            part,
-            pl.ds(pl.multiple_of(part * QTILE, QTILE), QTILE),
-            pl.ds(pl.multiple_of(head * HD, HD), HD),
-        )
-
-    def keys_of(k):
-        return kv[k, :, 0].reshape(2 * SPAN, HD)
-
-    def values_of(k):
-        return kv[k, :, 1].reshape(2 * SPAN, HD)
-
     shard = 2 * unit + core
 
-    def forward(n, carry):
-        part, rows, lanes = tile(n)
-        q = qd[0, rows, lanes]
-        g = qd[1, rows, lanes]
-        top = jnp.full((1, QTILE), NEGATIVE, f32)
-        for k in range(WINDOW):
-            at = slice(2 * SPAN * k, 2 * SPAN * (k + 1))
-            s = dot(keys_of(k), q, ((1,), (1,))) + bias[part, at, :]
-            e_buf[n, at, :] = s
-            top = jnp.maximum(top, jnp.max(s, axis=0, keepdims=True))
-        total = jnp.zeros((1, QTILE), f32)
-        slope = jnp.zeros((1, QTILE), f32)
-        for k in range(WINDOW):
-            at = slice(2 * SPAN * k, 2 * SPAN * (k + 1))
-            dp = dot(values_of(k), g, ((1,), (1,)))
-            e = jnp.exp2((e_buf[n, at, :] - top) * KAPPA)
+    def forward(half):
+        at = slice(WINDOW * SPAN * half, WINDOW * SPAN * (half + 1))
+        keys = kv[half, :, 0].reshape(WINDOW * SPAN, HD)
+        values = kv[half, :, 1].reshape(WINDOW * SPAN, HD)
+        for n in range(QSTEPS):
+            head, part = n // 2, n % 2
+            rows = slice(part * QTILE, (part + 1) * QTILE)
+            lanes = slice(head * HD, (head + 1) * HD)
+            s = dot(keys, qd[0, rows, lanes], ((1,), (1,))) + bias[part, at, :]
+            dp = dot(values, qd[1, rows, lanes], ((1,), (1,)))
+            top = jnp.max(s, axis=0, keepdims=True)
+            e = jnp.exp2((s - top) * KAPPA)
             e_buf[n, at, :] = e
             dp_buf[n, at, :] = dp
-            total = total + jnp.sum(e, axis=0, keepdims=True)
-            slope = slope + jnp.sum(e * dp, axis=0, keepdims=True)
-        stat[shard, 0, pl.ds(n, 1), :] = top
-        stat[shard, 1, pl.ds(n, 1), :] = total
-        stat[shard, 2, pl.ds(n, 1), :] = slope
-        return carry
-
-    stat[shard] = jnp.zeros(stat.shape[1:], f32)
-    lax.fori_loop(0, QSTEPS, forward, 0)
-
+            half_stat[half, 0, n : n + 1, :] = top
+            half_stat[half, 1, n : n + 1, :] = jnp.sum(e, axis=0, keepdims=True)
+            half_stat[half, 2, n : n + 1, :] = jnp.sum(e * dp, axis=0, keepdims=True)
+
+    half_stat[...] = jnp.zeros(half_stat.shape, f32)
+    for half in range(2):
+        for k in range(1, WINDOW):
+
+            @pl.when(chunk - k >= 0)
+            def _():
+                arrived(kv.at[half, k], kv_recv_sem.at[half, k])
+        forward(half)
+    def combined(parts):
+        top = jnp.max(parts[:, 0], axis=0)
+        factors = jnp.exp2((parts[:, 0] - top[None]) * KAPPA)
+        return (
+            top,
+            jnp.sum(parts[:, 1] * factors, axis=0),
+            jnp.sum(parts[:, 2] * factors, axis=0),
+        )
+
+    for i, row in enumerate(combined(half_stat[...])):
+        stat[shard, i] = row
     for sem, to in ((0, mate), (1, sibling), (2, mate + 1 - 2 * core)):
         sent.append(
             send(
@@ -307,13 +314,10 @@
     for step in range(1, 4):
         peer = (shard + step) % 4
         arrived(stat.at[peer], stat_recv_sem.at[peer])
-
-    tops = stat[:, 0]
-    top = jnp.max(tops, axis=0)
-    factors = jnp.exp2((tops - top[None]) * KAPPA)
-    inverse = 1.0 / jnp.maximum(jnp.sum(stat[:, 1] * factors, axis=0), TINY)
-    delta = jnp.sum(stat[:, 2] * factors, axis=0) * inverse
-    ratio = jnp.exp2((stat[shard, 0] - top) * KAPPA) * inverse
+    top, total, slope = combined(stat[...])
+    inverse = 1.0 / jnp.maximum(total, TINY)
+    delta = slope * inverse
+    ratios = [jnp.exp2((half_stat[half, 0] - top) * KAPPA) * inverse for half in range(2)]
 
     def dkv_copy(k, half):
         return pltpu.make_async_remote_copy(
@@ -324,19 +328,24 @@
             device_id=holder(chunk - k, half),
             device_id_type=MESH,
         )
-
-    for k in (4, 3, 2, 1, 0):
-        at = slice(2 * SPAN * k, 2 * SPAN * (k + 1))
+    for k in (2, 3, 1, 4, 0):
         dk = jnp.zeros((2 * SPAN, HD), f32)
         dv = jnp.zeros((2 * SPAN, HD), f32)
         for n in range(QSTEPS):
             head, part = n // 2, n % 2
             rows = slice(part * QTILE, (part + 1) * QTILE)
             lanes = slice(head * HD, (head + 1) * HD)
-            p = e_buf[n, at, :] * ratio[n : n + 1]
-            ds = (p * (dp_buf[n, at, :] - delta[n : n + 1])).astype(bf16)
-            ds_buf[n, at, :] = ds
-            dv = dv + dot(p.astype(bf16), qd[1, rows, lanes], ((1,), (0,)))
+            p_halves, ds_halves = [], []
+            for half in range(2):
+                at = slice((WINDOW * half + k) * SPAN, (WINDOW * half + k + 1) * SPAN)
+                p = e_buf[n, at, :] * ratios[half][n : n + 1]
+                ds = (p * (dp_buf[n, at, :] - delta[n : n + 1])).astype(bf16)
+                ds_buf[n, at, :] = ds
+                p_halves.append(p.astype(bf16))
+                ds_halves.append(ds)
+            p = jnp.concatenate(p_halves, axis=0)
+            ds = jnp.concatenate(ds_halves, axis=0)
+            dv = dv + dot(p, qd[1, rows, lanes], ((1,), (0,)))
             dk = dk + dot(ds, qd[0, rows, lanes], ((1,), (0,)))
         dk = dk * SCALE
         if k == 0:
@@ -368,7 +377,6 @@
             @pl.when(apart == k)
             def _():
                 dkv_recv[1, k] = dkv_send[k, 1]
-
     keys = kv[:, :, 0].reshape(2 * SPAN * WINDOW, HD)
     for n in range(QSTEPS):
         head, part = n // 2, n % 2
@@ -388,7 +396,6 @@
             )
         )
     dq_recv[is_back, shard] = dq_send[rows_of(own_block), :]
-
     def add_arrived(half, there, k, total):
         @pl.when(there & (apart != k) if half == 1 else there)
         def _():
@@ -408,7 +415,6 @@
         add_arrived(1, other_chunk + k < chunks, k, dkv_own)
     dk_out[other_rows, :] = dkv_own[0].astype(bf16)
     dv_out[other_rows, :] = dkv_own[1].astype(bf16)
-
     for step in range(1, 8):
         source = (place + step) % 8
         source_x = source // 2
@@ -423,7 +429,6 @@
         for j in range(1, 4):
             total_dq = total_dq + dq_recv[back, j].astype(f32)
         dq_out[back * SPAN : (back + 1) * SPAN, :] = total_dq.astype(bf16)
-
     for copy in sent:
         copy.wait_send()
     for k in range(1, WINDOW):
@@ -432,6 +437,7 @@
         def _():
             for half in range(2):
                 kv_copy(k, half).wait_send()
+    for k in range(1, WINDOW):
 
         @pl.when(chunk - k >= 0)
         def _():
@@ -475,10 +481,11 @@
         scratch_shapes=[
             vmem((2, CHUNK, HEADS * HD), bf16),
             vmem((2, SPAN, HEADS * HD), bf16),
-            vmem((WINDOW, 2, 2, SPAN, HD), bf16),
+            vmem((2, WINDOW, 2, SPAN, HD), bf16),
             vmem((2, SPAN, HD), bf16),
             vmem((positions // 128, 128), jnp.int32),
             vmem((CHUNK // QTILE, keys, QTILE), f32),
+            vmem((2, 3, 8, QTILE), f32),
             vmem((QSTEPS, keys, QTILE), f32),
             vmem((QSTEPS, keys, QTILE), f32),
             vmem((QSTEPS, keys, QTILE), bf16),
@@ -488,14 +495,16 @@
             vmem((2, SPAN, HD), f32),
             vmem((WINDOW, 2, 2, SPAN, HD), bf16),
             vmem((2, WINDOW, 2, SPAN, HD), bf16),
+            pltpu.SemaphoreType.REGULAR,
+            pltpu.SemaphoreType.REGULAR,
             sem((8,)),
             sem,
             sem((7,)),
             sem((8,)),
             sem,
             sem,
-            sem((WINDOW, 2)),
-            sem((WINDOW, 2)),
+            sem((2, WINDOW)),
+            sem((2, WINDOW)),
             sem((3,)),
             sem((4,)),
             sem((8,)),

time: 40.3 us -> 38.1 us (0.945)
  the two profiles are of different devices: /device:TPU:57 before, /device:TPU:1 now
where the time goes in v4:
time: 38.1 us; the launch traced here: 38 us
  Pallas kernels  37.4 us (98%)
  between operations  0.64 us (2%)
    pallas_call x1, Pallas kernels, local(): pl.pallas_call(functools.partial(kernel, slabs_per_group, slabs, 32), out...  35.8 us
    pallas_call x1, Pallas kernels, local(): pl.pallas_call(write_out, out_shape=shapes, in_specs=[pl.BlockSpec(memory...  1.6 us

profile of v4, /device:TPU:1, one launch (start us, length us, event | category | flops | bytes accessed | tf_op | source)
XLA Modules:
  0.0 38.0 jit_solution(15044321812230105614)
XLA Ops:
  0.6 35.8 %windowed_backward.1 = (bf16[128,384]{1,0:T(8,128)(2,1)}, bf16[128,128]{1,0:T(8,128)(2,1)}, bf16[128,128]{1,0:T(8,128)(2,1)}) custom-call(bf16[128,384]{1,0:T(8,128)(2,1)} %q_hbm.1, bf16[128,128]{1,0:T(8,128)(2,1)} %k_hbm.1, bf16[128,128]{1,0:T(8,128)(2,1)} %v_hbm.1, bf16[128,384]{1,0:T(8,128)(2,1)} %g_hbm.1, s32[256,128]{1,0:T(8,128)} %bitcast.1), custom_call_target="tpu_custom_call" | custom-call | tf_op jit(solution)/shard_map/windowed_backward/pallas_call | solution.py:476
  36.4 1.6 %write_out.1 = (bf16[128,384]{1,0:T(8,128)(2,1)}, bf16[128,128]{1,0:T(8,128)(2,1)}, bf16[128,128]{1,0:T(8,128)(2,1)}) custom-call(bf16[128,384]{1,0:T(8,128)(2,1)} %get-tuple-element.6.dq, bf16[128,128]{1,0:T(8,128)(2,1)} %get-tuple-element.7.dk, bf16[128,128]{1,0:T(8,128)(2,1)} %get-tuple-element.8.dv), custom_call_target="tpu_custom_call" | custom-call | tf_op jit(solution)/shard_map/write_out/pallas_call | solution.py:520

commit v5 on v4

--- a/solution.py
+++ b/solution.py
@@ -51,7 +51,9 @@
     dp_buf,
     ds_buf,
     stat,
-    dq_send,
+    dq_part,
+    dq_sib,
+    dq_sum,
     dq_recv,
     dkv_own,
     dkv_send,
@@ -68,6 +70,8 @@
     kv_recv_sem,
     stat_send_sem,
     stat_recv_sem,
+    dq_sib_send_sem,
+    dq_sib_recv_sem,
     dq_send_sem,
     dq_recv_sem,
     dkv_send_sem,
@@ -381,21 +385,38 @@
     for n in range(QSTEPS):
         head, part = n // 2, n % 2
         dqt = dot(keys, ds_buf[n], ((0,), (0,)))
-        dq_send[part * QTILE : (part + 1) * QTILE, head * HD : (head + 1) * HD] = (
-            dqt.T * SCALE
-        ).astype(bf16)
-    for step in (4, 2, 6, 3, 5, 7, 1):
-        to = (place + step) % 8
-        sent.append(
-            send(
-                dq_send.at[rows_of(block_of(to, is_back))],
-                dq_recv.at[is_back, shard],
-                dq_send_sem.at[step],
-                dq_recv_sem.at[is_back, shard],
-                in_slab(to),
+        rows_dq = (dqt.T * SCALE).astype(bf16)
+        for piece in range(QTILE // SPAN):
+            owner = block_of(part * (QTILE // SPAN) + piece, is_back)
+            dq_part[owner % 2, owner // 2, :, head * HD : (head + 1) * HD] = rows_dq[
+                piece * SPAN : (piece + 1) * SPAN
+            ]
+    sent.append(send(dq_part.at[1 - core], dq_sib, dq_sib_send_sem, dq_sib_recv_sem, in_slab(sibling)))
+    arrived(dq_sib, dq_sib_recv_sem)
+    for step in (2, 1, 3, 0):
+        to_x = (x + step) % 4
+        dq_sum[step] = (dq_part[core, to_x].astype(f32) + dq_sib[to_x].astype(f32)).astype(bf16)
+        if step > 0:
+            sent.append(
+                send(
+                    dq_sum.at[step],
+                    dq_recv.at[is_back, unit],
+                    dq_send_sem.at[step],
+                    dq_recv_sem.at[is_back, unit],
+                    in_slab(2 * to_x + core),
+                )
             )
-        )
-    dq_recv[is_back, shard] = dq_send[rows_of(own_block), :]
+    dq_recv[is_back, unit] = dq_sum[0]
+    for step in range(1, 4):
+        source_x = (x + step) % 4
+        source_back = source_x // 2
+        source_unit = jnp.where(source_back == 1, 3 - source_x, source_x)
+        arrived(
+            dq_recv.at[source_back, source_unit], dq_recv_sem.at[source_back, source_unit]
+        )
+    for back in range(2):
+        total_dq = dq_recv[back, 0].astype(f32) + dq_recv[back, 1].astype(f32)
+        dq_out[back * SPAN : (back + 1) * SPAN, :] = total_dq.astype(bf16)
     def add_arrived(half, there, k, total):
         @pl.when(there & (apart != k) if half == 1 else there)
         def _():
@@ -415,20 +436,6 @@
         add_arrived(1, other_chunk + k < chunks, k, dkv_own)
     dk_out[other_rows, :] = dkv_own[0].astype(bf16)
     dv_out[other_rows, :] = dkv_own[1].astype(bf16)
-    for step in range(1, 8):
-        source = (place + step) % 8
-        source_x = source // 2
-        source_back = source_x // 2
-        source_unit = jnp.where(source_back == 1, 3 - source_x, source_x)
-        source_shard = 2 * source_unit + source % 2
-        arrived(
-            dq_recv.at[source_back, source_shard], dq_recv_sem.at[source_back, source_shard]
-        )
-    for back in range(2):
-        total_dq = dq_recv[back, 0].astype(f32)
-        for j in range(1, 4):
-            total_dq = total_dq + dq_recv[back, j].astype(f32)
-        dq_out[back * SPAN : (back + 1) * SPAN, :] = total_dq.astype(bf16)
     for copy in sent:
         copy.wait_send()
     for k in range(1, WINDOW):
@@ -475,7 +482,7 @@
     )
     grads = pl.pallas_call(
         functools.partial(kernel, slabs_per_group, slabs, 32),
-        out_shape=shapes,
+        out_shape=tuple(pltpu.VMEM(shape.shape, shape.dtype) for shape in shapes),
         in_specs=[pl.BlockSpec(memory_space=pl.ANY)] * 5,
         out_specs=[pl.BlockSpec(memory_space=pltpu.VMEM)] * 3,
         scratch_shapes=[
@@ -490,8 +497,10 @@
             vmem((QSTEPS, keys, QTILE), f32),
             vmem((QSTEPS, keys, QTILE), bf16),
             vmem((4, 3, 8, QTILE), f32),
-            vmem((CHUNK, HEADS * HD), bf16),
             vmem((2, 4, SPAN, HEADS * HD), bf16),
+            vmem((4, SPAN, HEADS * HD), bf16),
+            vmem((4, SPAN, HEADS * HD), bf16),
+            vmem((2, 2, SPAN, HEADS * HD), bf16),
             vmem((2, SPAN, HD), f32),
             vmem((WINDOW, 2, 2, SPAN, HD), bf16),
             vmem((2, WINDOW, 2, SPAN, HD), bf16),
@@ -507,8 +516,10 @@
             sem((2, WINDOW)),
             sem((3,)),
             sem((4,)),
-            sem((8,)),
-            sem((2, 4)),
+            sem,
+            sem,
+            sem((4,)),
+            sem((2, 2)),
             sem((2, WINDOW)),
             sem((2, WINDOW)),
         ],
@@ -524,7 +535,7 @@
         out_specs=[pl.BlockSpec(memory_space=pl.ANY)] * 3,
         scratch_shapes=[sem((3,))],
         name="write_out",
-    )(*grads)
+    )(*(pltpu.with_memory_space_constraint(grad, pltpu.VMEM) for grad in grads))
 
 
 def solution(mesh):

time: 38.1 us -> 35.7 us (0.937)
  the two profiles are of different devices: /device:TPU:1 before, /device:TPU:25 now
where the time goes in v5:
time: 35.7 us; the launch traced here: 35.6 us
  Pallas kernels  35 us (98%)
  between operations  0.64 us (2%)
    pallas_call x1, Pallas kernels, local(): pl.pallas_call(functools.partial(kernel, slabs_per_group, slabs, 32), out...  34.3 us

profile of v5, /device:TPU:25, one launch (start us, length us, event | category | flops | bytes accessed | tf_op | source)
XLA Modules:
  0.0 35.6 jit_solution(4141554143583490336)
XLA Ops:
  0.6 34.3 %windowed_backward.1 = (bf16[128,384]{1,0:T(8,128)(2,1)S(1)}, bf16[128,128]{1,0:T(8,128)(2,1)S(1)}, bf16[128,128]{1,0:T(8,128)(2,1)S(1)}) custom-call(bf16[128,384]{1,0:T(8,128)(2,1)} %q_hbm.1, bf16[128,128]{1,0:T(8,128)(2,1)} %k_hbm.1, bf16[128,128]{1,0:T(8,128)(2,1)} %v_hbm.1, bf16[128,384]{1,0:T(8,128)(2,1)} %g_hbm.1, s32[256,128]{1,0:T(8,128)} %bitcast.1), custom_call_target="tpu_custom_call" | custom-call | tf_op jit(solution)/shard_map/windowed_backward/pallas_call | solution.py:483
  34.9 0.7 %write_out.1 = (bf16[128,384]{1,0:T(8,128)(2,1)}, bf16[128,128]{1,0:T(8,128)(2,1)}, bf16[128,128]{1,0:T(8,128)(2,1)}) custom-call(bf16[128,384]{1,0:T(8,128)(2,1)S(1)} %get-tuple-element.6.dq, bf16[128,128]{1,0:T(8,128)(2,1)S(1)} %get-tuple-element.7.dk, bf16[128,128]{1,0:T(8,128)(2,1)S(1)} %get-tuple-element.8.dv), custom_call_target="tpu_custom_call" | custom-call | tf_op jit(solution)/shard_map/write_out/pallas_call | solution.py:531

commit v6 on v5

--- a/solution.py
+++ b/solution.py
@@ -127,26 +127,26 @@
         pltpu.make_async_copy(q_hbm.at[own_rows], qd.at[0, rows_of(own_block)], local_sem.at[6]),
         pltpu.make_async_copy(g_hbm.at[own_rows], qd.at[1, rows_of(own_block)], local_sem.at[7]),
     ]
+    barrier = pltpu.get_barrier_semaphore()
+    for k in (2, 3, 1, 4):
+
+        @pl.when(chunk - k >= 0)
+        def _():
+            pl.semaphore_signal(
+                barrier, inc=1, device_id=holder(chunk - k, 0, 1), device_id_type=MESH
+            )
+
+    for step in range(4):
+        to_x = (x + step) % 4
+
+        @pl.when((step > 0) | (core == 1))
+        def _():
+            pl.semaphore_signal(barrier, inc=1, device_id=in_slab(2 * to_x), device_id_type=MESH)
+
     for copy in locals_:
         copy.start()
     seg_copy = pltpu.make_async_copy(seg_hbm, seg, seg_sem)
     seg_copy.start()
-
-    barrier = pltpu.get_barrier_semaphore()
-    for k in (2, 3, 1, 4):
-
-        @pl.when(chunk - k >= 0)
-        def _():
-            pl.semaphore_signal(
-                barrier, inc=1, device_id=holder(chunk - k, 0, 1), device_id_type=MESH
-            )
-
-    for step in range(4):
-        to_x = (x + step) % 4
-
-        @pl.when((step > 0) | (core == 1))
-        def _():
-            pl.semaphore_signal(barrier, inc=1, device_id=in_slab(2 * to_x), device_id_type=MESH)
 
     later = jnp.minimum(chunks - 1 - chunk, WINDOW - 1)
     apart = chunk - other_chunk
@@ -204,9 +204,9 @@
                 kv_copy(k, half).start()
 
     other_block = block_of(place, 1 - is_back)
+    sent.append(send_block(qd_other, other_block, 2, partner))
+    sent.append(send_block(qd_block(own_block), own_block, 1, mate))
     sent.append(send_block(qd_other, other_block, 0, far))
-    sent.append(send_block(qd_block(own_block), own_block, 1, mate))
-    sent.append(send_block(qd_other, other_block, 2, partner))
     sent.append(send_block(qd_block(own_block), own_block, 3, sibling))
 
     @pl.when(core == 1)
@@ -259,7 +259,7 @@
                 at = (WINDOW * half + k) * SPAN
                 bias[part, at : at + SPAN, :] = jnp.where(allowed, 0.0, NEGATIVE)
 
-    for sem, source in ((4, mate), (5, partner), (6, far)):
+    for sem, source in ((4, partner), (5, mate), (6, far)):
         block = block_of(source, is_back)
         arrived(qd_block(block), qd_recv_sem.at[block])
         sent.append(send_block(qd_block(block), block, sem, sibling))
@@ -305,7 +305,7 @@
 
     for i, row in enumerate(combined(half_stat[...])):
         stat[shard, i] = row
-    for sem, to in ((0, mate), (1, sibling), (2, mate + 1 - 2 * core)):
+    for sem, to in ((0, mate), (1, mate + 1 - 2 * core), (2, sibling)):
         sent.append(
             send(
                 stat.at[shard],
@@ -332,7 +332,7 @@
             device_id=holder(chunk - k, half),
             device_id_type=MESH,
         )
-    for k in (2, 3, 1, 4, 0):
+    for k in (3, 2, 1, 0, 4):
         dk = jnp.zeros((2 * SPAN, HD), f32)
         dv = jnp.zeros((2 * SPAN, HD), f32)
         for n in range(QSTEPS):
@@ -370,13 +370,13 @@
             dkv_send[k, :, 0] = dk.astype(bf16).reshape(2, SPAN, HD)
             dkv_send[k, :, 1] = dv.astype(bf16).reshape(2, SPAN, HD)
 
+            @pl.when((chunk - k >= 0) & (apart != k))
+            def _():
+                dkv_copy(k, 1).start()
+
             @pl.when(chunk - k >= 0)
             def _():
                 dkv_copy(k, 0).start()
-
-            @pl.when((chunk - k >= 0) & (apart != k))
-            def _():
-                dkv_copy(k, 1).start()
 
             @pl.when(apart == k)
             def _():

time: 35.7 us -> 34.5 us (0.966)
  the two profiles are of different devices: /device:TPU:25 before, /device:TPU:8 now
where the time goes in v6:
time: 34.5 us; the launch traced here: 34.4 us
  Pallas kernels  33.8 us (98%)
  between operations  0.64 us (2%)
    pallas_call x1, Pallas kernels, local(): pl.pallas_call(functools.partial(kernel, slabs_per_group, slabs, 32), out...  33.1 us

profile of v6, /device:TPU:8, one launch (start us, length us, event | category | flops | bytes accessed | tf_op | source)
XLA Modules:
  0.0 34.4 jit_solution(688584278837278092)
XLA Ops:
  0.6 33.1 %windowed_backward.1 = (bf16[128,384]{1,0:T(8,128)(2,1)S(1)}, bf16[128,128]{1,0:T(8,128)(2,1)S(1)}, bf16[128,128]{1,0:T(8,128)(2,1)S(1)}) custom-call(bf16[128,384]{1,0:T(8,128)(2,1)} %q_hbm.1, bf16[128,128]{1,0:T(8,128)(2,1)} %k_hbm.1, bf16[128,128]{1,0:T(8,128)(2,1)} %v_hbm.1, bf16[128,384]{1,0:T(8,128)(2,1)} %g_hbm.1, s32[256,128]{1,0:T(8,128)} %bitcast.1), custom_call_target="tpu_custom_call" | custom-call | tf_op jit(solution)/shard_map/windowed_backward/pallas_call | solution.py:483
  33.7 0.7 %write_out.1 = (bf16[128,384]{1,0:T(8,128)(2,1)}, bf16[128,128]{1,0:T(8,128)(2,1)}, bf16[128,128]{1,0:T(8,128)(2,1)}) custom-call(bf16[128,384]{1,0:T(8,128)(2,1)S(1)} %get-tuple-element.6.dq, bf16[128,128]{1,0:T(8,128)(2,1)S(1)} %get-tuple-element.7.dk, bf16[128,128]{1,0:T(8,128)(2,1)S(1)} %get-tuple-element.8.dv), custom_call_target="tpu_custom_call" | custom-call | tf_op jit(solution)/shard_map/write_out/pallas_call | solution.py:531

commit v7 on v6

--- a/solution.py
+++ b/solution.py
@@ -58,6 +58,7 @@
     dkv_own,
     dkv_send,
     dkv_recv,
+    keys_t,
     near_sem,
     far_sem,
     local_sem,
@@ -143,7 +144,7 @@
         def _():
             pl.semaphore_signal(barrier, inc=1, device_id=in_slab(2 * to_x), device_id_type=MESH)
 
-    for copy in locals_:
+    for copy in locals_[2:] + locals_[:2]:
         copy.start()
     seg_copy = pltpu.make_async_copy(seg_hbm, seg, seg_sem)
     seg_copy.start()
@@ -160,8 +161,6 @@
     def _():
         pl.semaphore_wait(near_sem, 1)
 
-    for copy in locals_:
-        copy.wait()
 
     def send(src, dst, send_sem, recv_sem, to):
         copy = pltpu.make_async_remote_copy(
@@ -184,6 +183,8 @@
     def send_block(src, block, sem, to):
         return send(src, qd_block(block), qd_send_sem.at[sem], qd_recv_sem.at[block], in_slab(to))
 
+    for copy in locals_[2:4]:
+        copy.wait()
     sent.append(send(kv_other, kv.at[1, 0], swap_send_sem, swap_recv_sem, in_slab(partner)))
 
     def kv_copy(k, half):
@@ -204,6 +205,8 @@
                 kv_copy(k, half).start()
 
     other_block = block_of(place, 1 - is_back)
+    for copy in locals_[:2] + locals_[4:]:
+        copy.wait()
     sent.append(send_block(qd_other, other_block, 2, partner))
     sent.append(send_block(qd_block(own_block), own_block, 1, mate))
     sent.append(send_block(qd_other, other_block, 0, far))
@@ -315,6 +318,7 @@
                 in_slab(to),
             )
         )
+    keys_t[...] = kv[:, :, 0].reshape(2 * SPAN * WINDOW, HD).T
     for step in range(1, 4):
         peer = (shard + step) % 4
         arrived(stat.at[peer], stat_recv_sem.at[peer])
@@ -381,10 +385,9 @@
             @pl.when(apart == k)
             def _():
                 dkv_recv[1, k] = dkv_send[k, 1]
-    keys = kv[:, :, 0].reshape(2 * SPAN * WINDOW, HD)
     for n in range(QSTEPS):
         head, part = n // 2, n % 2
-        dqt = dot(keys, ds_buf[n], ((0,), (0,)))
+        dqt = dot(keys_t[...], ds_buf[n], ((1,), (0,)))
         rows_dq = (dqt.T * SCALE).astype(bf16)
         for piece in range(QTILE // SPAN):
             owner = block_of(part * (QTILE // SPAN) + piece, is_back)
@@ -504,6 +507,7 @@
             vmem((2, SPAN, HD), f32),
             vmem((WINDOW, 2, 2, SPAN, HD), bf16),
             vmem((2, WINDOW, 2, SPAN, HD), bf16),
+            vmem((HD, keys), bf16),
             pltpu.SemaphoreType.REGULAR,
             pltpu.SemaphoreType.REGULAR,
             sem((8,)),

time: 34.5 us -> 34.5 us (level)
  no operation moved by 1% of the time
where the time goes in v7:
time: 34.5 us; the launch traced here: 34.4 us
  Pallas kernels  33.8 us (98%)
  between operations  0.64 us (2%)
    pallas_call x1, Pallas kernels, local(): pl.pallas_call(functools.partial(kernel, slabs_per_group, slabs, 32), out...  33.1 us

profile of v7, /device:TPU:8, one launch (start us, length us, event | category | flops | bytes accessed | tf_op | source)
XLA Modules:
  0.0 34.4 jit_solution(3760097133286690058)
XLA Ops:
  0.6 33.1 %windowed_backward.1 = (bf16[128,384]{1,0:T(8,128)(2,1)S(1)}, bf16[128,128]{1,0:T(8,128)(2,1)S(1)}, bf16[128,128]{1,0:T(8,128)(2,1)S(1)}) custom-call(bf16[128,384]{1,0:T(8,128)(2,1)} %q_hbm.1, bf16[128,128]{1,0:T(8,128)(2,1)} %k_hbm.1, bf16[128,128]{1,0:T(8,128)(2,1)} %v_hbm.1, bf16[128,384]{1,0:T(8,128)(2,1)} %g_hbm.1, s32[256,128]{1,0:T(8,128)} %bitcast.1), custom_call_target="tpu_custom_call" | custom-call | tf_op jit(solution)/shard_map/windowed_backward/pallas_call | solution.py:486
  33.7 0.7 %write_out.1 = (bf16[128,384]{1,0:T(8,128)(2,1)}, bf16[128,128]{1,0:T(8,128)(2,1)}, bf16[128,128]{1,0:T(8,128)(2,1)}) custom-call(bf16[128,384]{1,0:T(8,128)(2,1)S(1)} %get-tuple-element.6.dq, bf16[128,128]{1,0:T(8,128)(2,1)S(1)} %get-tuple-element.7.dk, bf16[128,128]{1,0:T(8,128)(2,1)S(1)} %get-tuple-element.8.dv), custom_call_target="tpu_custom_call" | custom-call | tf_op jit(solution)/shard_map/write_out/pallas_call | solution.py:535
